TPU v7x, 32 devices: a whole 2x2x4 slice. The times are simulated.
32 devices in a mesh: dp: 16 (over z, x, core), head: 2 (over y).
Axes of the slice: x: 2, y: 2, z: 4, core: 2. Of those that a mesh axis runs over, the one named last changes fastest.
Arguments:
- tokens: bfloat16 [16384, 768], P('dp'), may hold values from -6 to 6
- cotangent: bfloat16 [16384, 768], P(('dp', 'head')), may hold values from -6 to 6
- form_number: int32 [16, 1024], P('dp'), may hold values from 0 to 2, never falling along the last dimension, each value on 1 to 709 neighbouring positions
- sequence_bucket: int32 [16384, 1024], P('dp'), may hold values from 0 to 31
- horizontal_bucket: int32 [16384, 1024], P('dp'), may hold values from 0 to 63
- vertical_bucket: int32 [16384, 1024], P('dp'), may hold values from 0 to 63
- project_weight: bfloat16 [768, 3, 768], P(None, None, 'head'), may hold values from -0.21875 to 0.21875
- query_bias: bfloat16 [768], P('head'), may hold values from -3 to 3
- value_bias: bfloat16 [768], P('head'), may hold values from -3 to 3
- output_weight: bfloat16 [768, 768], P('head'), may hold values from -1.75 to 1.75
- output_bias: bfloat16 [768], replicated, may hold values from -3 to 3
- first_gain: bfloat16 [768], replicated, may hold values from 0.5 to 1.5
- first_shift: bfloat16 [768], replicated, may hold values from -2 to 2
- up_weight: bfloat16 [768, 3072], P(None, 'head'), may hold values from -0.21875 to 0.21875
- up_bias: bfloat16 [3072], P('head'), may hold values from -3 to 3
- down_weight: bfloat16 [3072, 768], P('head'), may hold values from -0.109375 to 0.109375
- down_bias: bfloat16 [768], replicated, may hold values from -3 to 3
- second_gain: bfloat16 [768], replicated, may hold values from 0.5 to 1.5
- second_shift: bfloat16 [768], replicated, may hold values from -2 to 2
- sequence_table: bfloat16 [32, 12], P(None, 'head'), may hold values from -4 to 4
- horizontal_table: bfloat16 [64, 12], P(None, 'head'), may hold values from -4 to 4
- vertical_table: bfloat16 [64, 12], P(None, 'head'), may hold values from -4 to 4
- project_weight_average: float32 [768, 3, 768], P('dp', None, 'head'), may hold values from -0.21875 to 0.21875
- query_bias_average: float32 [768], P('head'), may hold values from -3 to 3
- value_bias_average: float32 [768], P('head'), may hold values from -3 to 3
- output_weight_average: float32 [768, 768], P('head', 'dp'), may hold values from -1.75 to 1.75
- output_bias_average: float32 [768], replicated, may hold values from -3 to 3
- first_gain_average: float32 [768], replicated, may hold values from 0.5 to 1.5
- first_shift_average: float32 [768], replicated, may hold values from -2 to 2
- up_weight_average: float32 [768, 3072], P('dp', 'head'), may hold values from -0.21875 to 0.21875
- up_bias_average: float32 [3072], P('head'), may hold values from -3 to 3
- down_weight_average: float32 [3072, 768], P(('head', 'dp')), may hold values from -0.109375 to 0.109375
- down_bias_average: float32 [768], replicated, may hold values from -3 to 3
- second_gain_average: float32 [768], replicated, may hold values from 0.5 to 1.5
- second_shift_average: float32 [768], replicated, may hold values from -2 to 2
- sequence_table_average: float32 [32, 12], P(None, 'head'), may hold values from -4 to 4
- horizontal_table_average: float32 [64, 12], P(None, 'head'), may hold values from -4 to 4
- vertical_table_average: float32 [64, 12], P(None, 'head'), may hold values from -4 to 4
Outputs:
- layer_output: float32 [16384, 768], P(('dp', 'head'))
- tokens_gradient: float32 [16384, 768], P(('dp', 'head'))
- project_weight_gradient: float32 [768, 3, 768], P(None, None, 'head')
- query_bias_gradient: float32 [768], P('head')
- value_bias_gradient: float32 [768], P('head')
- output_weight_gradient: float32 [768, 768], P('head')
- output_bias_gradient: float32 [768], replicated
- first_gain_gradient: float32 [768], replicated
- first_shift_gradient: float32 [768], replicated
- up_weight_gradient: float32 [768, 3072], P(None, 'head')
- up_bias_gradient: float32 [3072], P('head')
- down_weight_gradient: float32 [3072, 768], P('head')
- down_bias_gradient: float32 [768], replicated
- second_gain_gradient: float32 [768], replicated
- second_shift_gradient: float32 [768], replicated
- sequence_table_gradient: float32 [32, 12], P(None, 'head')
- horizontal_table_gradient: float32 [64, 12], P(None, 'head')
- vertical_table_gradient: float32 [64, 12], P(None, 'head')
- project_weight_renewed: float32 [768, 3, 768], P('dp', None, 'head')
- query_bias_renewed: float32 [768], P('head')
- value_bias_renewed: float32 [768], P('head')
- output_weight_renewed: float32 [768, 768], P('head', 'dp')
- output_bias_renewed: float32 [768], replicated
- first_gain_renewed: float32 [768], replicated
- first_shift_renewed: float32 [768], replicated
- up_weight_renewed: float32 [768, 3072], P('dp', 'head')
- up_bias_renewed: float32 [3072], P('head')
- down_weight_renewed: float32 [3072, 768], P(('head', 'dp'))
- down_bias_renewed: float32 [768], replicated
- second_gain_renewed: float32 [768], replicated
- second_shift_renewed: float32 [768], replicated
- sequence_table_renewed: float32 [32, 12], P(None, 'head')
- horizontal_table_renewed: float32 [64, 12], P(None, 'head')
- vertical_table_renewed: float32 [64, 12], P(None, 'head')
Inputs may be any that keep to these rules, and one draw needn't show every extreme that they name: `form_number`: along each pack of 1024 positions the form numbers never fall; a form has at most min(709, 1024) positions, and some form has exactly that many.
All inputs are finite; a program needn't handle non-finite values.
Results may differ from a plain program's by a relative error of at most 0.014.
Values may be sent and summed in bfloat16 or wider, within the bound.
A program may use at most 256 MiB of HBM per device.

v0:
```python
import functools
import jax
import jax.numpy as jnp
from jax import lax
from jax.experimental import pallas as pl
from jax.sharding import PartitionSpec as P
from jax.experimental.pallas import tpu as pltpu

F32, BF16, I32 = jnp.float32, jnp.bfloat16, jnp.int32
SCALE_BITS = 27
STEP = 2.0**11
VM = 56 * 2**20
BACK_VM = 60 * 2**20
SAME = 2**17


def encode(buckets, same):
    seq, hor, ver = buckets
    return seq + 32 * hor + 2048 * ver + jnp.where(same, SAME, 0)


def buckets_of(code):
    return code & 31, (code >> 5) & 63, (code >> 11) & 63


def dot_nt(a, b):
    return lax.dot_general(a, b, (((1,), (1,)), ((), ())), preferred_element_type=F32)


def dot_tn(a, b):
    return lax.dot_general(a, b, (((0,), (0,)), ((), ())), preferred_element_type=F32)


def dot_general_t(w, x):
    return lax.dot_general(w, x, (((0,), (1,)), ((), ())), preferred_element_type=F32)


def dot_tt(a, b):
    return lax.dot_general(a, b, (((0,), (1,)), ((), ())), preferred_element_type=F32)


def dot_nn(a, b):
    return lax.dot_general(a, b, (((1,), (0,)), ((), ())), preferred_element_type=F32)


def split_pair(x):
    lane = lax.broadcasted_iota(I32, x.shape, 1)
    zero = jnp.zeros_like(x)
    return jnp.concatenate([jnp.where(lane < 64, x, zero), jnp.where(lane < 64, zero, x)], axis=0)


def partner(axis, bit):
    i = lax.axis_index(axis)
    low = lax.rem(lax.div(i, bit), 2)
    return {axis: i + bit * (1 - 2 * low)}


def dp_bit(bit):
    return lax.rem(lax.div(lax.axis_index("dp"), bit), 2)


def greet(partners):
    barrier = pltpu.get_barrier_semaphore()
    for p in partners:
        pl.semaphore_signal(barrier, inc=1, device_id=p, device_id_type=pl.DeviceIdType.MESH)
    pl.semaphore_wait(barrier, len(partners))


def remote(src, dst, send, recv, to):
    return pltpu.make_async_remote_copy(
        src_ref=src,
        dst_ref=dst,
        send_sem=send,
        recv_sem=recv,
        device_id=to,
        device_id_type=pl.DeviceIdType.MESH,
    )


def fetch_copies(mode, source, out, send, recv):
    if mode == "small":
        return [remote(source, out, send.at[0], recv.at[0], partner("head", 1)), None, None], []
    rows = source.shape[0] if mode == "rest" else source.shape[0] // 4
    quarter = 2 * dp_bit(1) + dp_bit(2)
    one = pl.ds(pl.multiple_of(quarter * rows, rows), rows)
    two = pl.ds(pl.multiple_of(dp_bit(1) * (2 * rows), 2 * rows), 2 * rows)
    hops, local = [None, None, None], []
    if mode == "first":
        hops[0] = remote(source.at[one], out, send.at[0], recv.at[0], partner("head", 1))
    else:
        if mode == "all":
            hops[0] = remote(source.at[one], out.at[one], send.at[0], recv.at[0], partner("head", 1))
            quarter_ref = out.at[one]
        else:
            quarter_ref = source
            local.append(pltpu.make_async_copy(source, out.at[one], send.at[0]))
        hops[1] = remote(quarter_ref, out.at[one], send.at[1], recv.at[1], partner("dp", 2))
        hops[2] = remote(out.at[two], out.at[two], send.at[2], recv.at[2], partner("dp", 1))
    return hops, local


def fetched_shape(mode, w):
    rows = {"all": 1, "small": 1, "first": 0.25, "rest": 4}[mode] * w.shape[0]
    return jax.ShapeDtypeStruct((int(rows), w.shape[1]), w.dtype)


def fwd_kernel(*refs, pairs, qb, modes, points, steps):
    n = len(modes)
    code, tab, q, kt, v = refs[:5]
    sources = refs[5 : 5 + n]
    p_out, c_out = refs[5 + n : 7 + n]
    outs = refs[7 + n : 7 + 2 * n]
    b_ref, t_ref, send, recv = refs[7 + 2 * n :]
    keys = v.shape[0]
    chunk = 128
    step = pl.program_id(0)
    hops, local = [], []
    for i in range(n):
        h, l = fetch_copies(modes[i], sources[i], outs[i], send.at[i], recv.at[i])
        hops.append(h)
        local += l

    def point(now):
        for i in range(n):
            for hop in range(3):
                if points[i][hop] == now:
                    if hop and hops[i][hop - 1] is not None:
                        hops[i][hop - 1].wait_recv()
                    hops[i][hop].start()

    @pl.when(step == 0)
    def _():
        greet([partner("head", 1), partner("dp", 2), partner("dp", 1)])
        for copy in local:
            copy.start()
        for j in range(pairs):
            for t in range(3):
                ls = slice(t * chunk, (t + 1) * chunk)
                fixed = [jnp.round(tab[2 * j + g : 2 * j + g + 1, ls] * STEP).astype(I32) for g in range(2)]
                t_ref[8 * (3 * j + t) : 8 * (3 * j + t) + 8, :] = jnp.broadcast_to(
                    fixed[0] * 65536 + fixed[1], (8, chunk)
                )
        point(0)

    for now in sorted(set(sum(points, ()))):
        if 0 < now < 2 * steps and now % 2 == 0:

            @pl.when(step == now // 2)
            def _():
                if local and now == min(p[2] for p, m in zip(points, modes) if m == "rest"):
                    for copy in local:
                        copy.wait()
                point(now)

    tbs = [t_ref[8 * i : 8 * i + 8, :] for i in range(3 * pairs)]

    def gather(r, _):
        rs = pl.ds(pl.multiple_of(r * 8, 8), 8)
        for c in range(keys // chunk):
            ls = slice(c * chunk, (c + 1) * chunk)
            sums = [None] * pairs
            for t, idx in enumerate(buckets_of(code[rs, ls])):
                for j in range(pairs):
                    g = jnp.take_along_axis(tbs[3 * j + t], idx, axis=1, mode="promise_in_bounds")
                    sums[j] = g if t == 0 else sums[j] + g
            for j in range(pairs):
                b_ref[j, rs, ls] = sums[j]
        return 0

    lax.fori_loop(0, qb // 8, gather, 0)
    for now in sorted(set(sum(points, ()))):
        if 0 < now < 2 * steps and now % 2 == 1:

            @pl.when(step == now // 2)
            def _():
                point(now)

    same = code[...] >= SAME
    def pair(j, _):
        lanes = pl.ds(pl.multiple_of(j * 128, 128), 128)
        q2 = split_pair(q[:, lanes])
        s2 = dot_nn(q2, kt[lanes, :])
        bias = b_ref[j]
        for g in range(2):
            x = s2[g * qb : (g + 1) * qb] + (bias << 16 if g else bias).astype(F32)
            x = jnp.where(same, x, -1e30)
            top = jnp.max(x, axis=1, keepdims=True)
            e = jnp.exp2((x - top) * (1.4426950408889634 * 2.0**-SCALE_BITS))
            inv = 1.0 / jnp.sum(e, axis=1, keepdims=True)
            p_out[2 * j + g] = (e * inv).astype(BF16)
        c0 = dot_nn(p_out[2 * j], v[:, lanes])
        c1 = dot_nn(p_out[2 * j + 1], v[:, lanes])
        lane = lax.broadcasted_iota(I32, c0.shape, 1)
        c_out[:, lanes] = jnp.where(lane < 64, c0, c1).astype(BF16)
        return 0

    lax.fori_loop(0, pairs, pair, 0)

    @pl.when(step == steps - 1)
    def _():
        for now in range(2 * steps, max(sum(points, ())) + 1):
            point(now)
        for i in range(n):
            last = [copy for copy in hops[i] if copy is not None][-1]
            last.wait_recv()
        for i in range(n):
            for copy in hops[i]:
                if copy is not None:
                    copy.wait_send()


def attend_fwd(code, tab, q, kt, v, fetch, collective_id, qb=128):
    nq, width = q.shape
    keys = v.shape[0]
    pairs = width // 128
    modes = tuple(f[0] for f in fetch)
    points = tuple(f[1] for f in fetch)
    sources = [f[2] for f in fetch]
    n = len(fetch)
    steps = nq // qb
    full = lambda a: pl.BlockSpec(a.shape, lambda i: (0,) * a.ndim)
    anywhere = pl.BlockSpec(memory_space=pl.ANY)
    return pl.pallas_call(
        functools.partial(fwd_kernel, pairs=pairs, qb=qb, modes=modes, points=points, steps=steps),
        out_shape=(
            jax.ShapeDtypeStruct((2 * pairs, nq, keys), BF16),
            jax.ShapeDtypeStruct((nq, width), BF16),
        )
        + tuple(fetched_shape(m, w) for m, w in zip(modes, sources)),
        grid=(steps,),
        in_specs=[
            pl.BlockSpec((qb, keys), lambda i: (i, 0)),
            full(tab),
            pl.BlockSpec((qb, width), lambda i: (i, 0)),
            full(kt),
            full(v),
        ]
        + [full(w) if m == "rest" else anywhere for m, w in zip(modes, sources)],
        out_specs=(
            pl.BlockSpec((2 * pairs, qb, keys), lambda i: (0, i, 0)),
            pl.BlockSpec((qb, width), lambda i: (i, 0)),
        )
        + (anywhere,) * n,
        scratch_shapes=[
            pltpu.VMEM((pairs, qb, keys), I32),
            pltpu.VMEM((pairs * 24, 128), I32),
            pltpu.SemaphoreType.DMA((n, 3)),
            pltpu.SemaphoreType.DMA((n, 3)),
        ],
        compiler_params=pltpu.CompilerParams(
            vmem_limit_bytes=VM, collective_id=collective_id, has_side_effects=True
        ),
        cost_estimate=pl.CostEstimate(
            flops=4 * nq * keys * width, bytes_accessed=90 * 2**20, transcendentals=nq * keys * 2 * pairs
        ),
    )(code, tab, q, kt, v, *sources)


def add_rows(dst, a, b, tile):
    rows = dst[2]

    def body(i, _):
        at = lambda x: pl.ds(pl.multiple_of(x[1] + i * tile, 16), tile)
        dst[0][at(dst), :] = a[0][at(a), :] + b[0][at(b), :]
        return 0

    lax.fori_loop(0, rows // tile, body, 0)


STREAM_SEMS = 17
ORDER_BITS = {"x": 2, "0": 4, "1": 8}


def stream_phases(own, other, kept, piece, full, columns, bufs, send, recv, order):
    half = own.shape[0] // 2
    tile = half // 8
    c = dp_bit(1)
    cut = lambda ref, start, n: ref.at[pl.ds(pl.multiple_of(start, 16), n), columns]
    part = lambda ref, bit, n: ref.at[pl.ds(pl.multiple_of(bit * n, 16), n)]
    hops = [
        [
            remote(cut(g, (1 - c) * half, half), bufs[0].at[m], send.at[m], recv.at[m], partner("dp", 1))
            for m, g in enumerate((own, other))
        ]
    ]
    adds = [
        [
            (bufs[0].at[m], (bufs[0].at[m], 0), (kept[m], 0) if kept else (g.at[:, columns], c * half), half)
            for m, g in enumerate((own, other))
        ]
    ]
    keep = []
    if kept:
        keep = [
            pltpu.make_async_copy(cut(g, c * half, half), kept[m], send.at[15 + m])
            for m, g in enumerate((own, other))
        ]
    n, at, two = half, c * half, True
    spans, bits = [(at, n)], [1]
    for i, axis in enumerate(order):
        buf, before = bufs[i + 1], bufs[i]
        if axis == "y":
            two = False
            hops.append([remote(before.at[1], buf.at[0], send.at[2 + 2 * i], recv.at[2 + 2 * i], partner("head", 1))])
            adds.append([(buf.at[0], (buf.at[0], 0), (before.at[0], 0), n)])
        else:
            n = n // 2
            bit = ORDER_BITS[axis]
            b = dp_bit(bit)
            at = at + b * n
            spans.append((at, n))
            bits.append(bit)
            sems = [2 + 2 * i + m for m in range(2 if two else 1)]
            hops.append(
                [
                    remote(part(before.at[m], 1 - b, n), buf.at[m], send.at[k], recv.at[k], partner("dp", bit))
                    for m, k in enumerate(sems)
                ]
            )
            adds.append([(buf.at[m], (buf.at[m], 0), (before.at[m], b * n), n) for m in range(len(sems))])
    dst, a, b, n = adds[-1][0]
    adds[-1] = [(piece, a, b, n)]
    there = lambda start, n: full.at[pl.ds(pl.multiple_of(start, 16), n), columns]
    back = [remote(piece, there(*spans[-1]), send.at[10], recv.at[10], partner("dp", bits[-1]))]
    for i in range(1, 4):
        ref = there(*spans[-1 - i])
        back.append(remote(ref, ref, send.at[10 + i], recv.at[10 + i], partner("dp", bits[-1 - i])))
    local = pltpu.make_async_copy(piece, there(*spans[-1]), send.at[14])

    def first():
        for copy in hops[0] + keep:
            copy.start()

    def reduce(i):
        def phase():
            for copy in keep if i == 0 else ():
                copy.wait()
            for copy in hops[i]:
                copy.wait_recv()
            for dst, a, b, n in adds[i]:
                add_rows((dst, 0, n), a, b, tile)
            if i < 4:
                for copy in hops[i + 1]:
                    copy.start()
            else:
                local.start()
                back[0].start()

        return phase

    def gather(i):
        def phase():
            if i == 1:
                local.wait()
            back[i - 1].wait_recv()
            back[i].start()

        return phase

    def finish():
        back[3].wait_recv()
        for copy in sum(hops, []) + back:
            copy.wait_send()

    return [first, *(reduce(i) for i in range(5)), *(gather(i) for i in range(1, 4)), finish]


def stream_scratch(rows, columns, order, keep):
    n, two = rows // 2, 2
    shapes = [(2, n, columns)]
    for axis in order:
        if axis == "y":
            two = 1
        else:
            n = n // 2
        shapes.append((two, n, columns))
    shapes.append((n, columns))
    if keep:
        shapes += [(rows // 2, columns)] * 2
    return [pltpu.VMEM(s, BF16) for s in shapes] + [pltpu.SemaphoreType.DMA((STREAM_SEMS,))] * 2


def sum_phases(own, other, bufs, send, recv):
    to = [partner("head", 1)] + [partner("dp", b) for b in (1, 2, 4, 8)]
    hops = [
        remote(other if i == 0 else own.at[i - 1], bufs.at[i], send.at[i], recv.at[i], to[i])
        for i in range(5)
    ]

    def phase(i):
        def run():
            if i:
                hops[i - 1].wait_recv()
                if i > 1:
                    own[i - 1] = own[i - 2] + bufs[i - 1]
                else:
                    own[0] = own[5] + bufs[0]
            if i < 5:
                hops[i].start()
            else:
                for copy in hops:
                    copy.wait_send()

        return run

    return [phase(i) for i in range(6)]


def attend_back(q, k, vt, do, p, ds, at, dq, dk, dv, pairs, qb):
    def pair(j, _):
        lanes = pl.ds(pl.multiple_of(j * 128, 128), 128)
        q2 = split_pair(q[:, lanes])
        do2 = split_pair(do[:, lanes])
        dp2 = dot_nn(do2, vt[lanes, :])
        parts = []
        for g in range(2):
            ps = p[2 * j + g].astype(F32)
            ts = ps * dp2[g * qb : (g + 1) * qb]
            inner = jnp.sum(ts, axis=1, keepdims=True)
            parts.append((ts - ps * inner).astype(BF16))
            ds[2 * j + g, pl.ds(at, qb), :] = parts[g]
        d0 = dot_nn(parts[0], k[:, lanes])
        d1 = dot_nn(parts[1], k[:, lanes])
        lane = lax.broadcasted_iota(I32, d0.shape, 1)
        dq[pl.ds(at, qb), lanes] = jnp.where(lane < 64, d0, d1).astype(BF16) * jnp.array(0.125, BF16)
        dk[lanes, :] += dot_tn(q2, jnp.concatenate(parts, axis=0))
        p2 = jnp.concatenate([p[2 * j], p[2 * j + 1]], axis=0)
        dv[lanes, :] += dot_tn(do2, p2)
        return 0

    lax.fori_loop(0, pairs, pair, 0)


def count_rows(code, ds, at, outs, bits, nq):
    heads = ds.shape[0]

    def rows(r, _):
        rs = pl.ds(pl.multiple_of(at + r * 16, 16), 16)
        dfull = [ds[h, rs, :].astype(F32) for h in range(heads)]
        for half in range(2):
            d8 = [d[half * 8 : half * 8 + 8] for d in dfull]
            packed = code[pl.ds(pl.multiple_of(r * 16 + half * 8, 8), 8), :]
            low = 0
            for t in range(3):
                signs = [(((packed << (31 - low - i)) >> 31) | 1).astype(F32) for i in range(bits[t])]
                low += bits[t]
                rhs = jnp.concatenate(
                    [jnp.concatenate([d, d * signs[0]], axis=0).astype(BF16) for d in d8], axis=0
                )
                first = jnp.concatenate([jnp.ones_like(signs[1]), signs[1]], axis=0).astype(BF16)
                tiles = [first]
                for i in range(2, bits[t]):
                    s2 = jnp.concatenate([signs[i], signs[i]], axis=0).astype(BF16)
                    tiles = tiles + [x * s2 for x in tiles]
                outs[t][...] += dot_nt(jnp.concatenate(tiles, axis=0), rhs)
        return 0

    lax.fori_loop(0, nq // 16, rows, 0)


def table_sums(acc, bits, first, heads):
    n = 2**bits
    high = lax.Precision.HIGHEST
    iota = lambda shape, d: lax.broadcasted_iota(I32, shape, d)
    row, col = iota(acc.shape, 0), iota(acc.shape, 1)
    kept = jnp.where((row & 7) == (col & 7), acc, 0.0)
    shape = (n, acc.shape[0])
    odd = (iota(shape, 1) >> 3) & (iota(shape, 0) >> 1)
    odd = odd ^ (odd >> 4)
    odd = odd ^ (odd >> 2)
    odd = odd ^ (odd >> 1)
    left = (1 - 2 * (odd & 1)).astype(F32)
    shape = (n, acc.shape[1])
    odd = iota(shape, 0) & (iota(shape, 1) >> 3) & 1
    mixed = jnp.dot(left, kept, precision=high, preferred_element_type=F32)
    mixed = mixed * (1 - 2 * odd).astype(F32) * (1.0 / n)
    shape = (8, acc.shape[1])
    head = iota(shape, 0)
    pick = ((iota(shape, 1) >> 4) == head + first) & (head < heads)
    return lax.dot_general(
        pick.astype(F32), mixed, (((1,), (1,)), ((), ())), precision=high, preferred_element_type=F32
    )


def back_kernel(*refs, pairs, qb, hb, steps, bits, fast, chunks, plan):
    refs = list(refs)
    take = lambda n: [refs.pop(0) for _ in range(n)]
    sides = [take(5), take(5)]
    code, xt, *weights = take(4)
    down_all, up_all, out_own, out_other, pre_own, pre_other = take(6)
    hidden = up_all.shape[2]
    down_own, down_other = down_all.at[0:hidden], down_all.at[hidden : 2 * hidden]
    up_own, up_other = up_all.at[0], up_all.at[1]
    full_down, full_up, full_out, full_project = take(4) if fast else [None] * 4
    token_out, sum_out = take(2)
    if fast:
        token_far = None
    else:
        token_far, sum_far = take(2)
        project = take(2)
    ds, dk, dv, dq, dkt, dvt = take(6)
    accs = take(3)
    if fast:
        project = take(2)
        token_far, token_near = take(2)
        sums, sum_other, sum_bufs = take(3)
        token_send, sum_send, sum_recv = take(3)
    step = pl.program_id(0)
    width = 2 * pairs * 64
    nq = qb * steps
    model = xt.shape[0]
    h = lax.axis_index("head")
    near = pl.ds(pl.multiple_of(h * nq, nq), nq)
    far = pl.ds(pl.multiple_of((1 - h) * nq, nq), nq)
    last = 2 * steps + 2 + (steps * qb) // hb

    if fast:
        phases = []
        sources = []
        down_chunks, up_chunks = chunks[:2]
        for own, other, full, pieces in (
            (down_own, down_other, full_down, down_chunks),
            (up_own, up_other, full_up, up_chunks),
        ):
            cols = own.shape[1] // pieces
            for i in range(pieces):
                sources.append((own, other, full, slice(i * cols, (i + 1) * cols), True))
        sources.append((out_own, out_other, full_out, slice(0, width), False))
        for start, stop in chunks[2]:
            sources.append((project[0], project[1], full_project, slice(start, stop), False))
        assert all(slot <= steps for slot, stream, phase in plan[0] if stream < down_chunks and phase < 2)
        cols = down_own.shape[1] // down_chunks
        per = 3 * width // cols
        spare = [project[i // per].at[:, i % per * cols : (i % per + 1) * cols] for i in range(2 * down_chunks)]
        for n, (own, other, full, columns, keep) in enumerate(sources):
            bufs = take(5)
            (piece,) = take(1)
            kept = None
            if keep:
                kept = spare[2 * n : 2 * n + 2] if n < down_chunks else take(2)
            send, recv = take(2)
            phases.append(
                stream_phases(own, other, kept, piece, full, columns, bufs, send, recv, plan[1][n])
            )
        token_hop = remote(token_far, token_near, token_send.at[0], token_send.at[1], partner("head", 1))

        def token_end():
            token_hop.wait_recv()
            token_out[...] = token_out[...] + token_near[...].astype(F32)
            token_hop.wait_send()

        phases.append([token_hop.start, token_end])
        phases.append(sum_phases(sums, sum_other, sum_bufs, sum_send, sum_recv))

        @pl.when(step == 0)
        def _():
            greet([partner("head", 1)] + [partner("dp", b) for b in (1, 2, 4, 8)])

        for now in sorted(set(p[0] for p in plan[0])):
            if now < last:

                @pl.when(step == now)
                def _():
                    for slot, stream, phase in plan[0]:
                        if slot == now:
                            phases[stream][phase]()

    @pl.when(step == 0)
    def _():
        for o in accs:
            o[...] = jnp.zeros_like(o)

    for s in range(2):
        q, k, vt, do, p = sides[s]
        first = s * (steps + 1)

        @pl.when((step >= first) & (step < first + steps))
        def _():
            block = step - first

            @pl.when(block == 0)
            def _():
                dk[...] = jnp.zeros_like(dk)
                dv[...] = jnp.zeros_like(dv)

            at = pl.multiple_of(block * qb, qb)
            side_ds = ds.at[s * 2 * pairs : (s + 1) * 2 * pairs]
            attend_back(q, k, vt, do, p, side_ds, at, dq, dk, dv, pairs, qb)

        @pl.when(step == first + steps)
        def _():
            dkt[...] = (dk[...] * 2.0**-SCALE_BITS).astype(BF16)
            dvt[...] = dv[...].astype(BF16)
            w = weights[s]
            wq, wk, wv = (w[i * model : (i + 1) * model, :] for i in range(3))
            project[s][:, :width] = dot_nn(xt[:, near], dq[...]).astype(BF16)
            project[s][:, width : 2 * width] = dot_nt(xt[...], dkt[...]).astype(BF16)
            project[s][:, 2 * width :] = dot_nt(xt[...], dvt[...]).astype(BF16)
            mine = dot_nt(wq, dq[...]) + dot_nn(wk, dkt[:, near]) + dot_nn(wv, dvt[:, near])
            theirs = dot_nn(wk, dkt[:, far]) + dot_nn(wv, dvt[:, far])
            if s:
                token_out[...] += mine
                token_far[...] = (token_far[...].astype(F32) + theirs).astype(BF16)
            else:
                token_out[...] = mine
                token_far[...] = theirs.astype(BF16)
            bias = sum_other if fast and s else sums.at[5] if fast else sum_far if s else sum_out
            ones = jnp.ones((8, nq), BF16)
            bias[8:16, :] = dot_nn(ones, dq[...])
            ones = jnp.ones((8, xt.shape[1]), BF16)
            bias[16:24, :] = dot_nt(ones, dvt[...])

    @pl.when(step >= 2 * steps + 2)
    def _():
        count_rows(code, ds, (step - 2 * steps - 2) * hb, accs, bits, hb)

    @pl.when(step == last - 1)
    def _():
        if fast:
            outs = (sums.at[5], sum_other)
        else:
            outs = (sum_out, sum_far)
        heads = 2 * pairs
        for s, o in enumerate(outs):
            o[0:8, :] = jnp.zeros((8, width), F32)
            for t, (acc, b) in enumerate(zip(accs, bits)):
                o[0:8, t * 128 : t * 128 + 2**b] = table_sums(acc[...], b, s * heads, heads)
            o[24:, :] = (pre_other if s else pre_own)[...]
        if fast:
            for slot, stream, phase in plan[0]:
                if slot >= last:
                    phases[stream][phase]()
            sum_out[...] = sums[4]


def attend_backward(sides, code, xt, weights, bits, grads, pre, collective_id, fast, plan, chunks, qb=128, hb=64):
    nq, width = sides[0][0].shape
    keys = sides[0][1].shape[0]
    model = xt.shape[0]
    pairs = width // 128
    heads = 2 * pairs
    steps = nq // qb
    ratio = qb // hb
    full = lambda shape: pl.BlockSpec(shape, lambda i: (0,) * len(shape), pipeline_mode=pl.Buffered(1))
    anywhere = pl.BlockSpec(memory_space=pl.ANY)
    in_specs, operands = [], []
    for s in range(2):
        clip = lambda i, s=s: jnp.clip(i - s * (steps + 1), 0, steps - 1)
        row = pl.BlockSpec((qb, width), lambda i, clip=clip: (clip(i), 0))
        big = pl.BlockSpec((heads, qb, keys), lambda i, clip=clip: (0, clip(i), 0))
        in_specs += [row, full((keys, width)), full((width, keys)), row, big]
        operands += list(sides[s])
    in_specs.append(
        pl.BlockSpec((hb, keys), lambda i: (jnp.clip(i - 2 * steps - 2, 0, steps * ratio - 1), 0))
    )
    in_specs += [full(a.shape) for a in (xt, *weights)]
    in_specs += [anywhere] * 2 + [full(a.shape) for a in (*grads[2:], *pre)]
    operands += [code, xt, *weights, *grads, *pre]
    sum_shape = (24 + pre[0].shape[0], width)
    project_shape = (model, 3 * width)
    shapes, out_specs = [], []
    if fast:
        hidden = grads[1].shape[2]
        shapes += [((hidden, model), BF16), ((model, hidden), BF16), ((model, width), BF16), (project_shape, BF16)]
        out_specs += [anywhere] * 4
    shapes += [((model, nq), F32), (sum_shape, F32)]
    if not fast:
        shapes += [((model, nq), BF16), (sum_shape, F32)] + [(project_shape, BF16)] * 2
    out_specs += [full(s) for s, _ in shapes[len(out_specs) :]]
    scratch = [
        pltpu.VMEM((2 * heads, nq, keys), BF16),
        pltpu.VMEM((width, keys), F32),
        pltpu.VMEM((width, keys), F32),
        pltpu.VMEM((nq, width), BF16),
        pltpu.VMEM((width, keys), BF16),
        pltpu.VMEM((width, keys), BF16),
    ] + [pltpu.VMEM((2 ** (b - 1) * 8, 2 * heads * 16), F32) for b in bits]
    params = dict(vmem_limit_bytes=BACK_VM)
    if fast:
        scratch += [pltpu.VMEM(project_shape, BF16)] * 2
        scratch += [pltpu.VMEM((model, nq), BF16)] * 2
        scratch += [pltpu.VMEM((6, *sum_shape), F32), pltpu.VMEM(sum_shape, F32)]
        scratch += [pltpu.VMEM((5, *sum_shape), F32)]
        scratch += [pltpu.SemaphoreType.DMA((2,)), pltpu.SemaphoreType.DMA((5,)), pltpu.SemaphoreType.DMA((5,))]
        n = 0
        for rows, columns, pieces in ((hidden, model, chunks[0]), (model, hidden, chunks[1])):
            for _ in range(pieces):
                scratch += stream_scratch(rows, columns // pieces, plan[1][n], n >= chunks[0])
                n += 1
        scratch += stream_scratch(model, width, plan[1][n], False)
        for start, stop in chunks[2]:
            n += 1
            scratch += stream_scratch(model, stop - start, plan[1][n], False)
        params.update(collective_id=collective_id, has_side_effects=True)
    return pl.pallas_call(
        functools.partial(
            back_kernel, pairs=pairs, qb=qb, hb=hb, steps=steps, bits=bits, fast=fast, chunks=chunks, plan=plan
        ),
        out_shape=tuple(jax.ShapeDtypeStruct(s, t) for s, t in shapes),
        grid=(2 * steps + 2 + steps * ratio,),
        in_specs=in_specs,
        out_specs=tuple(out_specs),
        scratch_shapes=scratch,
        compiler_params=pltpu.CompilerParams(**params),
        cost_estimate=pl.CostEstimate(
            flops=16 * nq * keys * width, bytes_accessed=300 * 2**20, transcendentals=0
        ),
    )(*operands)


norm_epsilon = 1e-05


def mm(a, b):
    return jnp.dot(a, b, preferred_element_type=F32)


def normalize(value):
    center = value - jnp.mean(value, axis=-1, keepdims=True)
    spread = jnp.mean(center * center, axis=-1, keepdims=True)
    root = lax.rsqrt(spread + norm_epsilon)
    return center * root, root


def normalize_back(grad, normed, root):
    return root * (
        grad
        - jnp.mean(grad, axis=-1, keepdims=True)
        - normed * jnp.mean(grad * normed, axis=-1, keepdims=True)
    )


def gelu_parts(u):
    t = 1.0 / (1.0 + (0.3275911 * 0.7071067811865476) * jnp.abs(u))
    e = jnp.exp(-0.5 * u * u)
    poly = t * (
        0.254829592 + t * (-0.284496736 + t * (1.421413741 + t * (-1.453152027 + t * 1.061405429)))
    )
    tail = 0.5 * e * poly
    below = jnp.where(u >= 0, 1.0 - tail, tail)
    return u * below, below + u * (e * 0.3989422804014327)


def swap_dp(x, bit):
    n = lax.axis_size("dp")
    return lax.ppermute(x, "dp", [(i, i ^ bit) for i in range(n)])


def swap_head(x):
    return lax.ppermute(x, "head", [(0, 1), (1, 0)])


def dp_bits():
    n, bit, out = lax.axis_size("dp"), 1, []
    while bit < n:
        out.append(bit)
        bit *= 2
    return out


def bit_of(bit):
    return (lax.axis_index("dp") // bit) % 2


def in_order(first, mine, theirs):
    low = jnp.where(first == 0, mine, theirs)
    high = jnp.where(first == 0, theirs, mine)
    return jnp.concatenate([low, high], axis=0)


def rows_of(x, index, rows):
    return lax.dynamic_slice_in_dim(x, index * rows, rows, 0)


def halve(g, bit):
    rows = g.shape[0] // 2
    b = bit_of(bit)
    got = swap_dp(rows_of(g, 1 - b, rows), bit)
    return (rows_of(g, b, rows).astype(F32) + got.astype(F32)).astype(BF16)


def reduce_grad(own, other, head_first):
    bits = dp_bits()
    own, other = halve(own, 1), halve(other, 1)
    if not head_first:
        own, other = halve(own, 2), halve(other, 2)
    g = (own.astype(F32) + swap_head(other).astype(F32)).astype(BF16)
    for bit in bits[1 if head_first else 2 :]:
        g = halve(g, bit)
    for bit in reversed(bits):
        g = in_order(bit_of(bit), g, swap_dp(g, bit))
    return g.astype(F32)


BACK_CHUNKS = (2, 2, ((0, 640), (640, 1152)))
BACK_PLAN = (
    ((0, 0, 0), (0, 1, 0), (0, 2, 0), (0, 3, 0), (0, 4, 0), (2, 0, 1), (3, 1, 1), (4, 2, 1), (5, 3, 1), (6, 0, 2), (6, 4, 1), (7, 1, 2), (8, 2, 2), (9, 0, 3), (10, 6, 0), (10, 7, 0), (10, 5, 0), (10, 0, 4), (10, 3, 2), (10, 1, 3), (10, 2, 3), (11, 0, 5), (11, 6, 1), (11, 4, 2), (12, 0, 6), (12, 5, 1), (12, 1, 4), (12, 3, 3), (12, 2, 4), (13, 0, 7), (13, 1, 5), (14, 7, 1), (14, 6, 2), (14, 2, 5), (15, 1, 6), (15, 4, 3), (15, 3, 4), (15, 0, 8), (15, 5, 2), (16, 0, 9), (16, 6, 3), (16, 2, 6), (16, 1, 7), (16, 3, 5), (17, 6, 4), (17, 5, 3), (17, 4, 4), (17, 3, 6), (18, 8, 0), (18, 6, 5), (18, 5, 4), (18, 2, 7), (18, 1, 8), (18, 8, 1), (18, 3, 7), (18, 6, 6), (18, 1, 9), (18, 8, 2), (18, 5, 5), (18, 4, 5), (18, 2, 8), (18, 3, 8), (18, 5, 6), (18, 8, 3), (18, 6, 7), (18, 4, 6), (18, 2, 9), (18, 8, 4), (18, 5, 7), (18, 3, 9), (18, 4, 7), (18, 8, 5), (18, 6, 8), (18, 5, 8), (18, 6, 9), (18, 4, 8), (18, 5, 9), (18, 4, 9)),
    ('x0y1', '0yx1', 'y0x1', 'x0y1', 'xy01', '0xy1', 'x0y1'),
)


def row_sums(x):
    return jnp.sum(x, axis=0, keepdims=True)


def ffn_kernel(
    x, cot, ctx_a, ctx_b, ow_a, ow_b, params, small_a, small_b, uw_a, uw_b, dw_a, dw_b,
    out, first, do_a, do_b, go_a, go_b, pre_a, pre_b, gd_all, gu_all,
    uw, dw, act, slope, gd, gu, total, bias, bias_sum, sem_in, sem_out,
    *, heads, chunk,
):
    width = ctx_a.shape[1]
    model = x.shape[1]
    hidden = uw_a.shape[1]
    per = hidden // chunk
    for s, (u, d) in enumerate(((uw_a, dw_a), (uw_b, dw_b))):
        for i in range(per):
            n = s * per + i
            cols = slice(i * chunk, (i + 1) * chunk)
            pltpu.make_async_copy(u.at[:, cols], uw.at[n], sem_in.at[n]).start()
            pltpu.make_async_copy(d.at[cols, :], dw.at[n], sem_in.at[2 * per + n]).start()
            small = (small_a, small_b)[s]
            for j in range(chunk // width):
                at = heads + 2 + i * (chunk // width) + j
                bias[n * 8 : n * 8 + 1, j * width : (j + 1) * width] = small[at : at + 1, :]
    gain1, shift1, gain2, shift2, output_shift, down_shift = (params[i : i + 1, :] for i in range(6))

    def put(i, vector):
        for o in (pre_a, pre_b):
            for n in range(model // width):
                o[i * (model // width) + n : i * (model // width) + n + 1, :] = vector[
                    :, n * width : (n + 1) * width
                ]

    attend = dot_nn(ctx_a[...], ow_a[...]) + dot_nn(ctx_b[...], ow_b[...]) + output_shift
    n1, root1 = normalize(x[...].astype(F32) + attend)
    normed = n1 * gain1 + shift1
    low = normed.astype(BF16)
    total[...] = normed + down_shift

    def forward(n, _):
        pltpu.make_async_copy(uw.at[n], uw.at[n], sem_in.at[n]).wait()
        row = bias[pl.ds(pl.multiple_of(n * 8, 8), 8), :][0:1]
        a, slope_n = gelu_parts(dot_nn(low, uw[n]) + row)
        a = a.astype(BF16)
        act[n] = a
        slope[n] = slope_n.astype(BF16)
        pltpu.make_async_copy(dw.at[n], dw.at[n], sem_in.at[2 * per + n]).wait()
        total[...] += dot_nn(a, dw[n])
        return 0

    lax.fori_loop(0, 2 * per, forward, 0)
    n2, root2 = normalize(total[...])
    out[...] = n2 * gain2 + shift2
    g = cot[...].astype(F32)
    put(2, row_sums(g * n2))
    put(3, row_sums(g))
    back = normalize_back(g * gain2, n2, root2)
    back_feed = back.astype(BF16)
    put(5, row_sums(back_feed.astype(F32)))
    total[...] = back

    def stores(n):
        rows = pl.ds(pl.multiple_of(n * chunk, chunk), chunk)
        cols = pl.ds(pl.multiple_of(lax.rem(n, per) * chunk, chunk), chunk)
        return (
            pltpu.make_async_copy(gd.at[n], gd_all.at[rows], sem_out.at[n]),
            pltpu.make_async_copy(gu.at[n], gu_all.at[lax.div(n, per), :, cols], sem_out.at[2 * per + n]),
        )

    def backward(n, _):
        gd[n] = dot_tn(act[n], back_feed).astype(BF16)
        stores(n)[0].start()
        back_up = (dot_nt(back_feed, dw[n]) * slope[n].astype(F32)).astype(BF16)
        bias_sum[pl.ds(pl.multiple_of(n * 8, 8), 8), :] = jnp.broadcast_to(
            row_sums(back_up.astype(F32)), (8, chunk)
        )
        gu[n] = dot_tn(low, back_up).astype(BF16)
        stores(n)[1].start()
        total[...] += dot_nt(back_up, uw[n])
        return 0

    lax.fori_loop(0, 2 * per, backward, 0)
    for n in range(2 * per):
        for j in range(chunk // width):
            at = 6 * (model // width) + (n % per) * (chunk // width) + j
            (pre_a, pre_b)[n // per][at : at + 1, :] = bias_sum[n * 8 : n * 8 + 1, j * width : (j + 1) * width]
    back = total[...]
    put(0, row_sums(back * n1))
    put(1, row_sums(back))
    back = normalize_back(back * gain1, n1, root1)
    first[...] = back
    back_attend = back.astype(BF16)
    put(4, row_sums(back_attend.astype(F32)))
    for ctx, ow, do, go in ((ctx_a, ow_a, do_a, go_a), (ctx_b, ow_b, do_b, go_b)):
        do[...] = dot_nt(back_attend, ow[...]).astype(BF16)
        go[...] = dot_tn(back_attend, ctx[...]).astype(BF16)
    for n in range(2 * per):
        for copy in stores(n):
            copy.wait()


def feed_forward(x, cot, contexts, output_weights, params, smalls, up_weights, down_weights, heads, chunk=768):
    nq, model = x.shape
    width = contexts[0].shape[1]
    hidden = up_weights[0].shape[1]
    n = 2 * hidden // chunk
    here = pl.BlockSpec(memory_space=pltpu.VMEM)
    anywhere = pl.BlockSpec(memory_space=pl.ANY)
    pre_rows = 6 * (model // width) + hidden // width
    shape = jax.ShapeDtypeStruct
    return pl.pallas_call(
        functools.partial(ffn_kernel, heads=heads, chunk=chunk),
        out_shape=(
            shape((nq, model), F32),
            shape((nq, model), F32),
            shape((nq, width), BF16),
            shape((nq, width), BF16),
            shape((model, width), BF16),
            shape((model, width), BF16),
            shape((pre_rows, width), F32),
            shape((pre_rows, width), F32),
            shape((2 * hidden, model), BF16),
            shape((2, model, hidden), BF16),
        ),
        in_specs=[here] * 9 + [anywhere] * 4,
        out_specs=(here,) * 8 + (anywhere,) * 2,
        scratch_shapes=[
            pltpu.VMEM((n, model, chunk), BF16),
            pltpu.VMEM((n, chunk, model), BF16),
            pltpu.VMEM((n, nq, chunk), BF16),
            pltpu.VMEM((n, nq, chunk), BF16),
            pltpu.VMEM((n, chunk, model), BF16),
            pltpu.VMEM((n, model, chunk), BF16),
            pltpu.VMEM((nq, model), F32),
            pltpu.VMEM((n * 8, chunk), F32),
            pltpu.VMEM((n * 8, chunk), F32),
            pltpu.SemaphoreType.DMA((2 * n,)),
            pltpu.SemaphoreType.DMA((2 * n,)),
        ],
        compiler_params=pltpu.CompilerParams(vmem_limit_bytes=VM),
        cost_estimate=pl.CostEstimate(
            flops=12 * nq * model * 2 * hidden, bytes_accessed=100 * 2**20, transcendentals=nq * 4 * hidden
        ),
    )(x, cot, *contexts, *output_weights, params, *smalls, *up_weights, *down_weights)


def finish_kernel(index, *refs, count, heads, scale):
    refs = list(refs)
    take = lambda n: [refs.pop(0) for _ in range(n)]
    down, up, out, project = take(4)
    down_piece, up_piece, out_piece, project_piece = take(4)
    tokens_t, first, sums, params, small = take(5)
    project_w, out_w, up_w, down_w = take(4)
    project_a, query_a, value_a, out_a, out_shift_a, gain1_a, shift1_a = take(7)
    up_a, up_bias_a, down_a, down_shift_a, gain2_a, shift2_a, *table_a = take(9)
    tokens_o, project_o, query_o, value_o, out_o, out_shift_o, gain1_o, shift1_o = take(8)
    up_o, up_bias_o, down_o, down_shift_o, gain2_o, shift2_o, *table_o = take(9)
    project_r, query_r, value_r, out_r, out_shift_r, gain1_r, shift1_r = take(7)
    up_r, up_bias_r, down_r, down_shift_r, gain2_r, shift2_r, *table_r = take(9)
    thirds = project.shape[1] // 3
    wide = lambda ref: ref[...].astype(F32)
    renew = lambda average, weight, grad: 0.5 * average + 0.5 * (weight - grad * scale)

    down_o[...] = wide(down)
    up_o[...] = wide(up)
    out_o[...] = jnp.transpose(wide(out))
    for i in range(3):
        project_o[i] = project[:, i * thirds : (i + 1) * thirds].astype(F32)
    tokens_o[...] = first[...] + jnp.transpose(tokens_t[...])

    @pl.when(pl.program_id(0) == 0)
    def _():
        up_r[...] = renew(up_a[...], wide(up_w), wide(up_piece))
        down_r[...] = renew(down_a[...], wide(down_w), wide(down_piece))
        out_r[...] = renew(out_a[...], jnp.transpose(wide(out_w)), wide(out_piece))
        for i in range(3):
            project_r[i] = renew(project_a[i], project_w[i].astype(F32), project_piece[:, i * thirds : (i + 1) * thirds].astype(F32))
        width = sums.shape[1]

        def vector(ref, at, n):
            return jnp.concatenate([ref[at + i : at + i + 1, :] for i in range(n)], axis=1)

        def flat(o, r, a, weight, grad):
            n = a.shape[0]
            o[...] = grad.reshape(n)
            r[...] = renew(a[...], weight.reshape(n), grad.reshape(n))

        flat(query_o, query_r, query_a, small[heads : heads + 1, :], sums[8:9, :])
        flat(value_o, value_r, value_a, small[heads + 1 : heads + 2, :], sums[16:17, :])
        two = params.shape[1] // width
        commons = (
            (gain1_o, gain1_r, gain1_a),
            (shift1_o, shift1_r, shift1_a),
            (gain2_o, gain2_r, gain2_a),
            (shift2_o, shift2_r, shift2_a),
            (out_shift_o, out_shift_r, out_shift_a),
            (down_shift_o, down_shift_r, down_shift_a),
        )
        for i, (o, r, a) in enumerate(commons):
            flat(o, r, a, params[i : i + 1, :], vector(sums, 24 + two * i, two))
        many = up_bias_a.shape[0] // width
        flat(
            up_bias_o, up_bias_r, up_bias_a, vector(small, heads + 2, many), vector(sums, 24 + 6 * two, many)
        )
        for t, (o, r, a) in enumerate(zip(table_o, table_r, table_a)):
            n = a.shape[1]
            grad = sums[0:heads, t * 128 : t * 128 + n]
            o[...] = grad
            r[...] = renew(a[...], small[0:heads, t * 128 : t * 128 + n], grad)


def finish(index, totals, tokens_t, first, sums, params, small, weights, averages, count, tokens_count, heads):
    swap = lambda a: a.transpose(1, 0, 2) if a.ndim == 3 else a.T
    turned = (0, 3, 13, 14, 15)
    averages = [swap(a) if i in turned else a for i, a in enumerate(averages)]
    down, up, out, project = totals
    model = first.shape[1]
    nq = first.shape[0]
    width = project.shape[1] // 3
    steps = model // 128
    full = lambda a: pl.BlockSpec(a.shape, lambda i, d: (0,) * len(a.shape))
    rows = lambda a: pl.BlockSpec((a.shape[0] // steps, a.shape[1]), lambda i, d: (i, 0))
    piece = lambda a: pl.BlockSpec(
        (a.shape[0] // count, *a.shape[1:]), lambda i, d: (d[0],) + (0,) * (len(a.shape) - 1)
    )
    columns = lambda n: pl.BlockSpec((n, 128), lambda i, d: (0, i))
    shape = lambda s: jax.ShapeDtypeStruct(s, F32)
    project_w, out_w, up_w, down_w = weights
    in_specs = [rows(a) for a in totals] + [piece(a) for a in totals]
    in_specs += [rows(tokens_t), columns(nq), full(sums), full(params), full(small)]
    project_spec = pl.BlockSpec((3, model // count, width), lambda i, d: (0, d[0], 0))
    in_specs += [project_spec, full(out_w), piece(up_w), piece(down_w)] + [full(a) for a in averages]
    grads = [
        shape((3, model, width)), shape((width,)), shape((width,)), shape((width, model)), shape((model,)),
        shape((model,)), shape((model,)), shape(up.shape), shape((up.shape[1],)), shape(down.shape),
        shape((model,)), shape((model,)), shape((model,)), *(shape(a.shape) for a in averages[13:]),
    ]
    specs = [full(g) for g in grads]
    specs[0] = pl.BlockSpec((3, 128, width), lambda i, d: (0, i, 0))
    specs[3] = columns(width)
    specs[7] = rows(up)
    specs[9] = rows(down)
    tokens, *results = pl.pallas_call(
        functools.partial(finish_kernel, count=count, heads=heads, scale=1.0 / tokens_count),
        out_shape=(shape((nq, model)), *grads, *(shape(a.shape) for a in averages)),
        grid_spec=pltpu.PrefetchScalarGridSpec(
            num_scalar_prefetch=1,
            grid=(steps,),
            in_specs=in_specs,
            out_specs=(columns(nq), *specs, *(full(a) for a in averages)),
        ),
        compiler_params=pltpu.CompilerParams(vmem_limit_bytes=VM),
        cost_estimate=pl.CostEstimate(flops=2**24, bytes_accessed=40 * 2**20, transcendentals=0),
    )(index, *totals, *totals, tokens_t, first, sums, params, small, *weights, *averages)
    grads, renewed = results[:16], results[16:]
    grads = [swap(a) if i in turned and i != 3 else a for i, a in enumerate(grads)]
    return tokens, *grads, *(swap(a) if i in turned else a for i, a in enumerate(renewed))


def local(
    tokens,
    cotangent,
    form_number,
    sequence_bucket,
    horizontal_bucket,
    vertical_bucket,
    project_weight,
    query_bias,
    value_bias,
    output_weight,
    output_bias,
    first_gain,
    first_shift,
    up_weight,
    up_bias,
    down_weight,
    down_bias,
    second_gain,
    second_shift,
    sequence_table,
    horizontal_table,
    vertical_table,
    project_weight_average,
    query_bias_average,
    value_bias_average,
    output_weight_average,
    output_bias_average,
    first_gain_average,
    first_shift_average,
    up_weight_average,
    up_bias_average,
    down_weight_average,
    down_bias_average,
    second_gain_average,
    second_shift_average,
    sequence_table_average,
    horizontal_table_average,
    vertical_table_average,
):
    total_rows, model_width = tokens.shape
    local_width = project_weight.shape[2]
    local_heads = sequence_table.shape[1]
    hidden = up_weight.shape[1]
    share_rows = total_rows // lax.axis_size("head")
    head_index = lax.axis_index("head")
    share_start = head_index * share_rows
    block_rows = 128
    buckets = (sequence_bucket, horizontal_bucket, vertical_bucket)
    tables = (sequence_table, horizontal_table, vertical_table)
    bits = tuple((t.shape[0] - 1).bit_length() for t in tables)
    project_stack = project_weight.transpose(1, 0, 2)
    flat_project = project_stack.reshape(3 * model_width, local_width)

    params = jnp.concatenate(
        [first_gain, first_shift, second_gain, second_shift, output_bias, down_bias]
    ).reshape(6, model_width).astype(F32)
    lanes = [jnp.pad(t.T, ((0, 0), (0, local_width // 3 - t.shape[0]))) for t in tables]
    small = jnp.concatenate(
        [
            jnp.concatenate(lanes, axis=1),
            jnp.concatenate([query_bias, value_bias, up_bias]).reshape(-1, local_width),
        ],
        axis=0,
    ).astype(F32)
    small = jnp.pad(small, ((0, 16 - small.shape[0]), (0, 0)))
    smalls, project_weights = [small], [flat_project]
    output_weights, up_weights, down_weights = [output_weight], [up_weight], [down_weight]

    form_row = form_number.reshape(total_rows)
    form_own = lax.dynamic_slice_in_dim(form_row, share_start, share_rows, 0)
    code = encode(
        [rows_of(b, head_index, share_rows) for b in buckets], form_own[:, None] == form_row[None, :]
    )
    own_tokens = rows_of(tokens, head_index, share_rows)

    scaled, keys, values_t, probs, contexts = [], [], [], [], []
    for s in range(2):
        wq, wk, wv = (project_weights[s][i * model_width : (i + 1) * model_width] for i in range(3))
        bq = smalls[s][local_heads : local_heads + 1]
        bv = smalls[s][local_heads + 1 : local_heads + 2]
        q = ((mm(own_tokens, wq) + bq) * 0.125).astype(BF16)
        q = q * jnp.array(2.0**SCALE_BITS, BF16)
        k = mm(tokens, wk).astype(BF16)
        kt = dot_general_t(wk, tokens).astype(BF16)
        v = (mm(tokens, wv) + bv).astype(BF16)
        vt = (dot_general_t(wv, tokens) + bv.reshape(-1, 1)).astype(BF16)
        if s == 0:
            fetch = (
                ("small", (0, -1, -1), small),
                ("all", (0, 3, 7), flat_project),
                ("all", (0, 4, 7), output_weight),
                ("first", (0, -1, -1), up_weight),
            )
        else:
            fetch = (("rest", (-1, 0, 4), up_part), ("all", (0, 4, 8), down_weight))
        p, context, *fetched = attend_fwd(code, smalls[s], q, kt, v, fetch, s, qb=block_rows)
        if s == 0:
            smalls.append(fetched[0])
            project_weights.append(fetched[1])
            output_weights.append(fetched[2])
            up_part = fetched[3]
        else:
            up_weights.append(fetched[0])
            down_weights.append(fetched[1])
        scaled.append(q)
        keys.append(k)
        values_t.append(vt)
        probs.append(p)
        contexts.append(context)
    (
        layer_output, back_first, back_own, back_other, out_own, out_other, pre_own, pre_other, *grads
    ) = feed_forward(
        own_tokens, cotangent, contexts, output_weights, params, smalls, up_weights, down_weights, local_heads
    )

    sides = [
        (scaled[s], keys[s], values_t[s], (back_own, back_other)[s], probs[s]) for s in range(2)
    ]
    pre = (pre_own, pre_other)
    fast = lax.axis_size("dp") == 16
    results = attend_backward(
        sides,
        code,
        tokens.T,
        project_weights,
        bits,
        (*grads, out_own, out_other),
        pre,
        2,
        fast,
        BACK_PLAN,
        BACK_CHUNKS,
        qb=block_rows,
    )
    token_count = total_rows * lax.axis_size("dp")
    group_count = lax.axis_size("dp")
    group_index = lax.axis_index("dp")
    if fast:
        width = model_width // group_count
        output_piece = lax.dynamic_slice_in_dim(output_weight, group_index * width, width, 1)
        averages = (
            project_weight_average, query_bias_average, value_bias_average, output_weight_average,
            output_bias_average, first_gain_average, first_shift_average, up_weight_average, up_bias_average,
            down_weight_average, down_bias_average, second_gain_average, second_shift_average,
            sequence_table_average, horizontal_table_average, vertical_table_average,
        )
        return layer_output, *finish(
            jnp.full((1,), group_index, I32),
            results[:4],
            results[4],
            back_first,
            results[5],
            params,
            small,
            (project_stack, output_piece, up_weight, down_weight),
            averages,
            group_count,
            token_count,
            local_heads,
        )
    tokens_gradient, sums, far, sums_other = results[:4]
    tokens_gradient = tokens_gradient + swap_head(far).astype(F32)
    sums = sums + swap_head(sums_other)
    for bit in dp_bits():
        sums = sums + swap_dp(sums, bit)
    down_total, up_total = reduce_grad(grads[0][:hidden], grads[0][hidden:], True), reduce_grad(*grads[1], False)
    output_total = reduce_grad(out_own, out_other, True)
    project_total = reduce_grad(results[4], results[5], False)
    tokens_gradient = back_first + tokens_gradient.T
    project_total = project_total.reshape(model_width, 3, local_width)
    output_total = output_total.T
    query_bias_total, value_bias_total = sums[8], sums[16]
    tail = sums[24:].reshape(-1)
    (
        first_gain_total,
        first_shift_total,
        second_gain_total,
        second_shift_total,
        output_bias_total,
        down_bias_total,
    ) = (tail[i * model_width : (i + 1) * model_width] for i in range(6))
    up_bias_total = tail[6 * model_width :]
    sequence_total, horizontal_total, vertical_total = (
        sums[:local_heads, i * 128 : i * 128 + t.shape[0]].T for i, t in enumerate(tables)
    )
    up_weight_total, down_weight_total, output_weight_total = up_total, down_total, output_total

    def renew(average, weight, gradient):
        return 0.5 * average + 0.5 * (weight.astype(jnp.float32) - gradient / token_count)

    def part_of(array, along):
        width = array.shape[along] // group_count
        return lax.dynamic_slice_in_dim(array, group_index * width, width, along)

    return (
        layer_output,
        tokens_gradient,
        project_total,
        query_bias_total,
        value_bias_total,
        output_weight_total,
        output_bias_total,
        first_gain_total,
        first_shift_total,
        up_weight_total,
        up_bias_total,
        down_weight_total,
        down_bias_total,
        second_gain_total,
        second_shift_total,
        sequence_total,
        horizontal_total,
        vertical_total,
        renew(project_weight_average, part_of(project_weight, 0), part_of(project_total, 0)),
        renew(query_bias_average, query_bias, query_bias_total),
        renew(value_bias_average, value_bias, value_bias_total),
        renew(output_weight_average, part_of(output_weight, 1), part_of(output_weight_total, 1)),
        renew(output_bias_average, output_bias, output_bias_total),
        renew(first_gain_average, first_gain, first_gain_total),
        renew(first_shift_average, first_shift, first_shift_total),
        renew(up_weight_average, part_of(up_weight, 0), part_of(up_weight_total, 0)),
        renew(up_bias_average, up_bias, up_bias_total),
        renew(down_weight_average, part_of(down_weight, 0), part_of(down_weight_total, 0)),
        renew(down_bias_average, down_bias, down_bias_total),
        renew(second_gain_average, second_gain, second_gain_total),
        renew(second_shift_average, second_shift, second_shift_total),
        renew(sequence_table_average, sequence_table, sequence_total),
        renew(horizontal_table_average, horizontal_table, horizontal_total),
        renew(vertical_table_average, vertical_table, vertical_total),
    )


def solution(mesh):
    in_specs = (
        P("dp", None),
        P(("dp", "head"), None),
        P("dp", None),
        P("dp", None),
        P("dp", None),
        P("dp", None),
        P(None, None, "head"),
        P("head"),
        P("head"),
        P("head", None),
        P(),
        P(),
        P(),
        P(None, "head"),
        P("head"),
        P("head", None),
        P(),
        P(),
        P(),
        P(None, "head"),
        P(None, "head"),
        P(None, "head"),
        P("dp", None, "head"),
        P("head"),
        P("head"),
        P("head", "dp"),
        P(),
        P(),
        P(),
        P("dp", "head"),
        P("head"),
        P(("head", "dp"), None),
        P(),
        P(),
        P(),
        P(None, "head"),
        P(None, "head"),
        P(None, "head"),
    )
    out_specs = (
        P(("dp", "head"), None),
        P(("dp", "head"), None),
        P(None, None, "head"),
        P("head"),
        P("head"),
        P("head", None),
        P(),
        P(),
        P(),
        P(None, "head"),
        P("head"),
        P("head", None),
        P(),
        P(),
        P(),
        P(None, "head"),
        P(None, "head"),
        P(None, "head"),
        P("dp", None, "head"),
        P("head"),
        P("head"),
        P("head", "dp"),
        P(),
        P(),
        P(),
        P("dp", "head"),
        P("head"),
        P(("head", "dp"), None),
        P(),
        P(),
        P(),
        P(None, "head"),
        P(None, "head"),
        P(None, "head"),
    )
    return jax.shard_map(local, mesh=mesh, in_specs=in_specs, out_specs=out_specs, check_vma=False)
```

profile of v0, /device:TPU:0, one launch (start us, length us, event | category | flops | bytes accessed | tf_op | source)
XLA Modules:
  0.0 275.3 jit_solution(15093093344599889089)
XLA Ops:
  0.7 0.7 constant_dynamic-slice_fusion
  1.4 0.0 copy-start.8
  1.4 0.0 copy-start.9
  1.4 4.8 %select_add_fusion.refs_0_.refs_10_ = s32[512,1024]{1,0:T(8,128)} fusion(s32[1024,1024]{1,0:T(8,128)} %param.43, s32[]{:T(128)S(6)} %select_n.14, s32[1024,1024]{1,0:T(8,128)} %param.42, s32[1024,1024]{1,0:T(8,128)} %param.41, s32[1024]{0:T(1024)} %bitcast.58, s32[512]{0:T(512)S(1)} %bitcast.59), kind=kLoop, calls=%fused_computation | loop fusion | flops 3670016 | bytes 8394756 | tf_op jit(solution)/shard_map/add | solution.py:19
  6.3 0.9 constant_dynamic-slice_fusion.2.x
  7.3 2.5 fusion.5.refs_2_.refs_0_
  9.8 1.9 add_convert_fusion.2.refs_4_
  11.6 1.7 convolution_convert_fusion.2.refs_3_
  13.3 0.6 pad.18.refs_1_.refs_5_.small_a.refs_12_
  13.9 35.1 %shard_map.621 = (bf16[6,512,1024]{2,1,0:T(8,128)(2,1)}, bf16[512,384]{1,0:T(8,128)(2,1)}, f32[16,384]{1,0:T(8,128)}, bf16[2304,384]{1,0:T(8,128)(2,1)}, bf16[38...) custom-call(s32[512,1024]{1,0:T(8,128)} %select_add_fusion.refs_0_.refs_10_, ...), custom_call_target="tpu_custom_call" | custom-call | flops 805306368 | bytes 94371840 | tf_op jit(solution)/shard_map/pallas_call | solution.py:223
  49.1 0.8 slice_reduce_fusion.2
  49.9 2.4 fusion.4.refs_2_.refs_5_
  52.3 1.9 add_convert_fusion.1.refs_7_
  54.2 1.2 copy.74.refs_4_
  55.4 2.0 convolution_convert_fusion
  57.4 1.2 copy.73.refs_3_
  58.6 0.0 copy-start.14
  58.6 35.8 %shard_map.622 = (bf16[6,512,1024]{2,1,0:T(8,128)(2,1)}, bf16[512,384]{1,0:T(8,128)(2,1)}, bf16[768,1536]{1,0:T(8,128)(2,1)}, bf16[1536,768]{1,0:T(8,128)(2,1)}) custom-call(s32[512,1024]{1,0:T(8,128)} %select_add_fusion.refs_0_.refs_10_, f32[16,384]{1,0:T(8,128)} %get-tuple-element.94.refs_1_.small_b, bf16[512,384]{1,0:T(8,128)(2,1)} %fusion.4.refs_2_.refs_5_, ...), custom_call_target="tpu_custom_call" | custom-call | flops 805306368 | bytes 94371840 | tf_op jit(solution)/shard_map/pallas_call | solution.py:223
  94.5 0.2 dynamic-update-slice
  94.7 0.2 dynamic-update-slice.1
  94.9 0.2 dynamic-update-slice.2
  95.1 0.2 dynamic-update-slice.3
  95.3 0.2 dynamic-update-slice.4
  95.6 0.2 dynamic-update-slice.5
  95.8 0.6 reshape.90.params.refs_11_
  96.4 32.5 %shard_map.623 = (f32[512,768]{1,0:T(8,128)}, f32[512,768]{1,0:T(8,128)}, bf16[512,384]{1,0:T(8,128)(2,1)}, bf16[512,384]{1,0:T(8,128)(2,1)}, bf16[768,384]{1,0:...) custom-call(bf16[512,768]{1,0:T(8,128)(2,1)} %constant_dynamic-slice, ...), custom_call_target="tpu_custom_call" | custom-call | flops 14495514624 | bytes 104857600 | tf_op jit(solution)/shard_map/pallas_call | solution.py:912
  128.9 1.8 add_convert_fusion.refs_2_
  130.7 1.9 convolution_convert_fusion.1.refs_1_
  132.5 1.6 copy.75
  134.2 127.2 %shard_map.624 = (bf16[1536,768]{1,0:T(8,128)(2,1)}, bf16[768,1536]{1,0:T(8,128)(2,1)}, bf16[768,384]{1,0:T(8,128)(2,1)}, bf16[768,1152]{1,0:T(8,128)(2,1)}, f32[768,512]{1,0:T(8,128)}, /*index=5*/f32[40,384]{1,0:T(8,128)}) custom-call(bf16[512,384]{1,0:T(8,128)(2,1)} %fusion.5.refs_2_.refs_0_, bf16[1024,384]{1,0:T(8,128)(2,1)} %convolution_convert_fusion.1.refs_1_, ...), custom_call_target="tpu_custom_call" | custom-call | flops 3221225472 | bytes 314572800 | tf_op jit(solution)/shard_map/pallas_call | solution.py:695
  261.4 1.7 constant_dynamic-slice_fusion.1.refs_14_
  263.0 12.1 %shard_map.625 = (f32[512,768]{1,0:T(8,128)}, f32[3,768,384]{2,1,0:T(8,128)}, f32[384]{0:T(512)}, f32[384]{0:T(512)}, f32[384,768]{1,0:T(8,128)}, /*index=5*/f32...) custom-call(s32[1]{0:T(128)} %bitcast.11.index, ...), custom_call_target="tpu_custom_call" | custom-call | flops 16777216 | bytes 41943040 | tf_op jit(solution)/shard_map/pallas_call | solution.py:1044
  (38 shorter events, 0.1 us)
Async XLA Ops:
  1.4 4.9 %copy-start.2 = (bf16[1024,768]{1,0:T(8,128)(2,1)S(1)}, bf16[1024,768]{1,0:T(8,128)(2,1)}, u32[]{:S(2)}) copy-start(bf16[1024,768]{1,0:T(8,128)(2,1)} %param.38) | copy-start | bytes 4718596
  1.4 5.8 %copy-start.6 = (bf16[1536]{0:T(1024)(128)(2,1)S(1)}, bf16[1536]{0:T(1024)(128)(2,1)}, u32[]{:S(2)}) copy-start(bf16[1536]{0:T(1024)(128)(2,1)} %param.52) | copy-start | bytes 9220
  1.4 5.8 %copy-start.16 = (bf16[384]{0:T(512)(128)(2,1)S(1)}, bf16[384]{0:T(512)(128)(2,1)}, u32[]{:S(2)}) copy-start(bf16[384]{0:T(512)(128)(2,1)} %param.46) | copy-start | bytes 2308
  1.4 5.8 %copy-start.17 = (bf16[384]{0:T(512)(128)(2,1)S(1)}, bf16[384]{0:T(512)(128)(2,1)}, u32[]{:S(2)}) copy-start(bf16[384]{0:T(512)(128)(2,1)} %param.45) | copy-start | bytes 2308
  1.4 5.8 %copy-start.7 = (bf16[64,6]{0,1:T(8,128)(2,1)S(1)}, bf16[64,6]{0,1:T(8,128)(2,1)}, u32[]{:S(2)}) copy-start(bf16[64,6]{0,1:T(8,128)(2,1)} %param.59) | copy-start | bytes 2308
  1.4 5.8 %copy-start.8 = (bf16[64,6]{0,1:T(8,128)(2,1)S(1)}, bf16[64,6]{0,1:T(8,128)(2,1)}, u32[]{:S(2)}) copy-start(bf16[64,6]{0,1:T(8,128)(2,1)} %param.58) | copy-start | bytes 2308
  1.4 5.8 %copy-start.9 = (bf16[32,6]{0,1:T(8,128)(2,1)S(1)}, bf16[32,6]{0,1:T(8,128)(2,1)}, u32[]{:S(2)}) copy-start(bf16[32,6]{0,1:T(8,128)(2,1)} %param.57) | copy-start | bytes 1156
  1.4 5.9 %copy-start = (bf16[768,3,384]{2,0,1:T(8,128)(2,1)S(1)}, bf16[768,3,384]{2,0,1:T(8,128)(2,1)}, u32[]{:S(2)}) copy-start(bf16[768,3,384]{2,0,1:T(8,128)(2,1)} %param.44) | copy-start | bytes 5308420
  13.9 35.9 %copy-start.5 = (bf16[512,768]{1,0:T(8,128)(2,1)S(1)}, bf16[512,768]{1,0:T(8,128)(2,1)}, u32[]{:S(2)}) copy-start(bf16[512,768]{1,0:T(8,128)(2,1)} %constant_dynamic-slice_fusion.2.x) | copy-start | bytes 2359300
  54.2 3.2 %copy-start.3 = (bf16[384,1024]{1,0:T(8,128)(2,1)}, bf16[384,1024]{1,0:T(8,128)(2,1)S(1)}, u32[]{:S(2)}) copy-start(bf16[384,1024]{1,0:T(8,128)(2,1)S(1)} %add_convert_fusion.1.refs_7_) | copy-start | bytes 2359300
  57.4 37.0 %copy-start.4 = (bf16[384,1024]{0,1:T(8,128)(2,1)}, bf16[384,1024]{0,1:T(8,128)(2,1)S(1)}, u32[]{:S(2)}) copy-start(bf16[384,1024]{0,1:T(8,128)(2,1)S(1)} %convolution_convert_fusion) | copy-start | bytes 2359300
  58.6 35.8 %copy-start.10 = (bf16[768]{0:T(1024)(128)(2,1)S(1)}, bf16[768]{0:T(1024)(128)(2,1)}, u32[]{:S(2)}) copy-start(bf16[768]{0:T(1024)(128)(2,1)} %param.49) | copy-start | bytes 4612
  58.6 36.1 %copy-start.11 = (bf16[768]{0:T(1024)(128)(2,1)S(1)}, bf16[768]{0:T(1024)(128)(2,1)}, u32[]{:S(2)}) copy-start(bf16[768]{0:T(1024)(128)(2,1)} %param.50) | copy-start | bytes 4612
  58.6 36.3 %copy-start.12 = (bf16[768]{0:T(1024)(128)(2,1)S(1)}, bf16[768]{0:T(1024)(128)(2,1)}, u32[]{:S(2)}) copy-start(bf16[768]{0:T(1024)(128)(2,1)} %param.55) | copy-start | bytes 4612
  58.6 36.5 %copy-start.13 = (bf16[768]{0:T(1024)(128)(2,1)S(1)}, bf16[768]{0:T(1024)(128)(2,1)}, u32[]{:S(2)}) copy-start(bf16[768]{0:T(1024)(128)(2,1)} %param.56) | copy-start | bytes 4612
  58.6 36.7 %copy-start.14 = (bf16[768]{0:T(1024)(128)(2,1)S(1)}, bf16[768]{0:T(1024)(128)(2,1)}, u32[]{:S(2)}) copy-start(bf16[768]{0:T(1024)(128)(2,1)} %param.48) | copy-start | bytes 4612
  58.6 36.9 %copy-start.15 = (bf16[768]{0:T(1024)(128)(2,1)S(1)}, bf16[768]{0:T(1024)(128)(2,1)}, u32[]{:S(2)}) copy-start(bf16[768]{0:T(1024)(128)(2,1)} %param.54) | copy-start | bytes 4612
  96.4 32.5 %copy-start.1 = (bf16[768,3,384]{2,0,1:T(8,128)(2,1)S(1)}, bf16[768,3,384]{2,0,1:T(8,128)(2,1)}, u32[]{:S(2)}) copy-start(bf16[768,3,384]{2,0,1:T(8,128)(2,1)} %param.44) | copy-start | bytes 5308420
where the time goes:
time: 276 us; the launch traced here: 275 us
  Pallas kernels  243 us (88%)
  matrix products  16 us (6%)
  local copies, waits for them, and re-layouts  10.7 us (4%)
  other arithmetic  4.84 us (2%)
    pallas_call x1, Pallas kernels, attend_backward(): pl.pallas_call(functools.partial(back_kernel, pairs=pairs, qb=qb, hb=hb,...  127 us
    pallas_call x2, Pallas kernels, attend_fwd(): pl.pallas_call(functools.partial(fwd_kernel, pairs=pairs, qb=qb, modes=mo...  70.9 us
    pallas_call x1, Pallas kernels, feed_forward(): pl.pallas_call(functools.partial(ffn_kernel, heads=heads, chunk=chunk), o...  32.5 us
    pallas_call x1, Pallas kernels, finish(): pl.pallas_call(functools.partial(finish_kernel, count=count, heads=heads,...  12.1 us
    dot_general x5, matrix products, mm(): return jnp.dot(a, b, preferred_element_type=F32)  10.5 us

commit v1 on v0

--- a/solution.py
+++ b/solution.py
@@ -59,11 +59,15 @@
     return lax.rem(lax.div(lax.axis_index("dp"), bit), 2)
 
 
-def greet(partners):
+def announce(partners):
     barrier = pltpu.get_barrier_semaphore()
     for p in partners:
         pl.semaphore_signal(barrier, inc=1, device_id=p, device_id_type=pl.DeviceIdType.MESH)
-    pl.semaphore_wait(barrier, len(partners))
+
+
+def greet(partners):
+    announce(partners)
+    pl.semaphore_wait(pltpu.get_barrier_semaphore(), len(partners))
 
 
 def remote(src, dst, send, recv, to):
@@ -271,24 +275,21 @@
 ORDER_BITS = {"x": 2, "0": 4, "1": 8}
 
 
-def stream_phases(own, other, kept, piece, full, columns, bufs, send, recv, order):
-    half = own.shape[0] // 2
+def stream_phases(own, other, kept, piece, full, columns, bufs, send, recv, order, part_of=None):
+    rest = part_of == "rest"
+    half = (full if rest else own).shape[0] // 2
     tile = half // 8
     c = dp_bit(1)
     cut = lambda ref, start, n: ref.at[pl.ds(pl.multiple_of(start, 16), n), columns]
     part = lambda ref, bit, n: ref.at[pl.ds(pl.multiple_of(bit * n, 16), n)]
-    hops = [
-        [
-            remote(cut(g, (1 - c) * half, half), bufs[0].at[m], send.at[m], recv.at[m], partner("dp", 1))
-            for m, g in enumerate((own, other))
-        ]
-    ]
-    adds = [
-        [
-            (bufs[0].at[m], (bufs[0].at[m], 0), (kept[m], 0) if kept else (g.at[:, columns], c * half), half)
-            for m, g in enumerate((own, other))
-        ]
-    ]
+    hops, adds = [[]], [[]]
+    if not rest:
+        for m, g in enumerate((own, other)):
+            hops[0].append(
+                remote(cut(g, (1 - c) * half, half), bufs[0].at[m], send.at[m], recv.at[m], partner("dp", 1))
+            )
+            mine = (kept[m], 0) if kept else (g.at[:, columns], c * half)
+            adds[0].append((bufs[0].at[m], (bufs[0].at[m], 0), mine, half))
     keep = []
     if kept:
         keep = [
@@ -297,9 +298,18 @@
         ]
     n, at, two = half, c * half, True
     spans, bits = [(at, n)], [1]
-    for i, axis in enumerate(order):
+    for i, axis in enumerate(order[:1] if part_of == "head" else order):
         buf, before = bufs[i + 1], bufs[i]
-        if axis == "y":
+        if rest and i == 0:
+            two = axis != "y"
+            if two:
+                n = n // 2
+                at = at + dp_bit(ORDER_BITS[axis]) * n
+                spans.append((at, n))
+                bits.append(ORDER_BITS[axis])
+            hops.append([])
+            adds.append([])
+        elif axis == "y":
             two = False
             hops.append([remote(before.at[1], buf.at[0], send.at[2 + 2 * i], recv.at[2 + 2 * i], partner("head", 1))])
             adds.append([(buf.at[0], (buf.at[0], 0), (before.at[0], 0), n)])
@@ -318,14 +328,14 @@
                 ]
             )
             adds.append([(buf.at[m], (buf.at[m], 0), (before.at[m], b * n), n) for m in range(len(sems))])
-    dst, a, b, n = adds[-1][0]
-    adds[-1] = [(piece, a, b, n)]
-    there = lambda start, n: full.at[pl.ds(pl.multiple_of(start, 16), n), columns]
-    back = [remote(piece, there(*spans[-1]), send.at[10], recv.at[10], partner("dp", bits[-1]))]
-    for i in range(1, 4):
-        ref = there(*spans[-1 - i])
-        back.append(remote(ref, ref, send.at[10 + i], recv.at[10 + i], partner("dp", bits[-1 - i])))
-    local = pltpu.make_async_copy(piece, there(*spans[-1]), send.at[14])
+
+    def head():
+        for copy in hops[1]:
+            copy.wait_recv()
+        for dst, a, b, n in adds[1]:
+            add_rows((dst, 0, n), a, b, tile)
+        for copy in hops[0] + hops[1]:
+            copy.wait_send()
 
     def first():
         for copy in hops[0] + keep:
@@ -348,6 +358,17 @@
 
         return phase
 
+    if part_of == "head":
+        return [first, reduce(0), head]
+    dst, a, b, n = adds[-1][0]
+    adds[-1] = [(piece, a, b, n)]
+    there = lambda start, n: full.at[pl.ds(pl.multiple_of(start, 16), n), columns]
+    back = [remote(piece, there(*spans[-1]), send.at[10], recv.at[10], partner("dp", bits[-1]))]
+    for i in range(1, 4):
+        ref = there(*spans[-1 - i])
+        back.append(remote(ref, ref, send.at[10 + i], recv.at[10 + i], partner("dp", bits[-1 - i])))
+    local = pltpu.make_async_copy(piece, there(*spans[-1]), send.at[14])
+
     def gather(i):
         def phase():
             if i == 1:
@@ -365,7 +386,7 @@
     return [first, *(reduce(i) for i in range(5)), *(gather(i) for i in range(1, 4)), finish]
 
 
-def stream_scratch(rows, columns, order, keep):
+def stream_scratch(rows, columns, order, keep, rest=False):
     n, two = rows // 2, 2
     shapes = [(2, n, columns)]
     for axis in order:
@@ -375,6 +396,8 @@
             n = n // 2
         shapes.append((two, n, columns))
     shapes.append((n, columns))
+    if rest:
+        shapes = shapes[2:]
     if keep:
         shapes += [(rows // 2, columns)] * 2
     return [pltpu.VMEM(s, BF16) for s in shapes] + [pltpu.SemaphoreType.DMA((STREAM_SEMS,))] * 2
@@ -406,12 +429,12 @@
     return [phase(i) for i in range(6)]
 
 
-def attend_back(q, k, vt, do, p, ds, at, dq, dk, dv, pairs, qb):
+def attend_back(q, kt, v, do, p, ds, at, dq, dk, dv, pairs, qb):
     def pair(j, _):
         lanes = pl.ds(pl.multiple_of(j * 128, 128), 128)
         q2 = split_pair(q[:, lanes])
         do2 = split_pair(do[:, lanes])
-        dp2 = dot_nn(do2, vt[lanes, :])
+        dp2 = dot_nt(do2, v[:, lanes])
         parts = []
         for g in range(2):
             ps = p[2 * j + g].astype(F32)
@@ -419,8 +442,8 @@
             inner = jnp.sum(ts, axis=1, keepdims=True)
             parts.append((ts - ps * inner).astype(BF16))
             ds[2 * j + g, pl.ds(at, qb), :] = parts[g]
-        d0 = dot_nn(parts[0], k[:, lanes])
-        d1 = dot_nn(parts[1], k[:, lanes])
+        d0 = dot_nt(parts[0], kt[lanes, :])
+        d1 = dot_nt(parts[1], kt[lanes, :])
         lane = lax.broadcasted_iota(I32, d0.shape, 1)
         dq[pl.ds(at, qb), lanes] = jnp.where(lane < 64, d0, d1).astype(BF16) * jnp.array(0.125, BF16)
         dk[lanes, :] += dot_tn(q2, jnp.concatenate(parts, axis=0))
@@ -487,9 +510,9 @@
     take = lambda n: [refs.pop(0) for _ in range(n)]
     sides = [take(5), take(5)]
     code, xt, *weights = take(4)
-    down_all, up_all, out_own, out_other, pre_own, pre_other = take(6)
+    states = take(chunks[0]) if fast else []
+    up_all, out_own, out_other, pre_own, pre_other = take(5)
     hidden = up_all.shape[2]
-    down_own, down_other = down_all.at[0:hidden], down_all.at[hidden : 2 * hidden]
     up_own, up_other = up_all.at[0], up_all.at[1]
     full_down, full_up, full_out, full_project = take(4) if fast else [None] * 4
     token_out, sum_out = take(2)
@@ -518,30 +541,25 @@
         phases = []
         sources = []
         down_chunks, up_chunks = chunks[:2]
-        for own, other, full, pieces in (
-            (down_own, down_other, full_down, down_chunks),
-            (up_own, up_other, full_up, up_chunks),
-        ):
-            cols = own.shape[1] // pieces
-            for i in range(pieces):
-                sources.append((own, other, full, slice(i * cols, (i + 1) * cols), True))
-        sources.append((out_own, out_other, full_out, slice(0, width), False))
+        cols = model // down_chunks
+        for i in range(down_chunks):
+            sources.append((None, None, full_down, slice(i * cols, (i + 1) * cols)))
+        cols = hidden // up_chunks
+        for i in range(up_chunks):
+            sources.append((up_own, up_other, full_up, slice(i * cols, (i + 1) * cols)))
+        sources.append((out_own, out_other, full_out, slice(0, width)))
         for start, stop in chunks[2]:
-            sources.append((project[0], project[1], full_project, slice(start, stop), False))
-        assert all(slot <= steps for slot, stream, phase in plan[0] if stream < down_chunks and phase < 2)
-        cols = down_own.shape[1] // down_chunks
-        per = 3 * width // cols
-        spare = [project[i // per].at[:, i % per * cols : (i % per + 1) * cols] for i in range(2 * down_chunks)]
-        for n, (own, other, full, columns, keep) in enumerate(sources):
-            bufs = take(5)
+            sources.append((project[0], project[1], full_project, slice(start, stop)))
+        for n, (own, other, full, columns) in enumerate(sources):
+            rest = n < down_chunks
+            bufs = [None, states[n], *take(3)] if rest else take(5)
             (piece,) = take(1)
-            kept = None
-            if keep:
-                kept = spare[2 * n : 2 * n + 2] if n < down_chunks else take(2)
+            kept = take(2) if down_chunks <= n < down_chunks + up_chunks else None
             send, recv = take(2)
-            phases.append(
-                stream_phases(own, other, kept, piece, full, columns, bufs, send, recv, plan[1][n])
+            made = stream_phases(
+                own, other, kept, piece, full, columns, bufs, send, recv, plan[1][n], "rest" if rest else None
             )
+            phases.append(made)
         token_hop = remote(token_far, token_near, token_send.at[0], token_send.at[1], partner("head", 1))
 
         def token_end():
@@ -571,7 +589,7 @@
             o[...] = jnp.zeros_like(o)
 
     for s in range(2):
-        q, k, vt, do, p = sides[s]
+        q, kt, v, do, p = sides[s]
         first = s * (steps + 1)
 
         @pl.when((step >= first) & (step < first + steps))
@@ -585,7 +603,7 @@
 
             at = pl.multiple_of(block * qb, qb)
             side_ds = ds.at[s * 2 * pairs : (s + 1) * 2 * pairs]
-            attend_back(q, k, vt, do, p, side_ds, at, dq, dk, dv, pairs, qb)
+            attend_back(q, kt, v, do, p, side_ds, at, dq, dk, dv, pairs, qb)
 
         @pl.when(step == first + steps)
         def _():
@@ -635,7 +653,7 @@
 
 def attend_backward(sides, code, xt, weights, bits, grads, pre, collective_id, fast, plan, chunks, qb=128, hb=64):
     nq, width = sides[0][0].shape
-    keys = sides[0][1].shape[0]
+    keys = sides[0][1].shape[1]
     model = xt.shape[0]
     pairs = width // 128
     heads = 2 * pairs
@@ -648,19 +666,19 @@
         clip = lambda i, s=s: jnp.clip(i - s * (steps + 1), 0, steps - 1)
         row = pl.BlockSpec((qb, width), lambda i, clip=clip: (clip(i), 0))
         big = pl.BlockSpec((heads, qb, keys), lambda i, clip=clip: (0, clip(i), 0))
-        in_specs += [row, full((keys, width)), full((width, keys)), row, big]
+        in_specs += [row, full((width, keys)), full((keys, width)), row, big]
         operands += list(sides[s])
     in_specs.append(
         pl.BlockSpec((hb, keys), lambda i: (jnp.clip(i - 2 * steps - 2, 0, steps * ratio - 1), 0))
     )
     in_specs += [full(a.shape) for a in (xt, *weights)]
-    in_specs += [anywhere] * 2 + [full(a.shape) for a in (*grads[2:], *pre)]
+    in_specs += [full(a.shape) for a in grads[:-3]] + [anywhere] + [full(a.shape) for a in (*grads[-2:], *pre)]
     operands += [code, xt, *weights, *grads, *pre]
     sum_shape = (24 + pre[0].shape[0], width)
     project_shape = (model, 3 * width)
     shapes, out_specs = [], []
     if fast:
-        hidden = grads[1].shape[2]
+        hidden = grads[-3].shape[2]
         shapes += [((hidden, model), BF16), ((model, hidden), BF16), ((model, width), BF16), (project_shape, BF16)]
         out_specs += [anywhere] * 4
     shapes += [((model, nq), F32), (sum_shape, F32)]
@@ -685,7 +703,7 @@
         n = 0
         for rows, columns, pieces in ((hidden, model, chunks[0]), (model, hidden, chunks[1])):
             for _ in range(pieces):
-                scratch += stream_scratch(rows, columns // pieces, plan[1][n], n >= chunks[0])
+                scratch += stream_scratch(rows, columns // pieces, plan[1][n], n >= chunks[0], n < chunks[0])
                 n += 1
         scratch += stream_scratch(model, width, plan[1][n], False)
         for start, stop in chunks[2]:
@@ -792,10 +810,10 @@
     return g.astype(F32)
 
 
-BACK_CHUNKS = (2, 2, ((0, 640), (640, 1152)))
+BACK_CHUNKS = (3, 2, ((0, 384), (384, 768), (768, 1152)))
 BACK_PLAN = (
-    ((0, 0, 0), (0, 1, 0), (0, 2, 0), (0, 3, 0), (0, 4, 0), (2, 0, 1), (3, 1, 1), (4, 2, 1), (5, 3, 1), (6, 0, 2), (6, 4, 1), (7, 1, 2), (8, 2, 2), (9, 0, 3), (10, 6, 0), (10, 7, 0), (10, 5, 0), (10, 0, 4), (10, 3, 2), (10, 1, 3), (10, 2, 3), (11, 0, 5), (11, 6, 1), (11, 4, 2), (12, 0, 6), (12, 5, 1), (12, 1, 4), (12, 3, 3), (12, 2, 4), (13, 0, 7), (13, 1, 5), (14, 7, 1), (14, 6, 2), (14, 2, 5), (15, 1, 6), (15, 4, 3), (15, 3, 4), (15, 0, 8), (15, 5, 2), (16, 0, 9), (16, 6, 3), (16, 2, 6), (16, 1, 7), (16, 3, 5), (17, 6, 4), (17, 5, 3), (17, 4, 4), (17, 3, 6), (18, 8, 0), (18, 6, 5), (18, 5, 4), (18, 2, 7), (18, 1, 8), (18, 8, 1), (18, 3, 7), (18, 6, 6), (18, 1, 9), (18, 8, 2), (18, 5, 5), (18, 4, 5), (18, 2, 8), (18, 3, 8), (18, 5, 6), (18, 8, 3), (18, 6, 7), (18, 4, 6), (18, 2, 9), (18, 8, 4), (18, 5, 7), (18, 3, 9), (18, 4, 7), (18, 8, 5), (18, 6, 8), (18, 5, 8), (18, 6, 9), (18, 4, 8), (18, 5, 9), (18, 4, 9)),
-    ('x0y1', '0yx1', 'y0x1', 'x0y1', 'xy01', '0xy1', 'x0y1'),
+    ((0, 5, 0), (0, 2, 2), (0, 3, 0), (0, 4, 0), (0, 1, 2), (0, 0, 2), (1, 5, 1), (2, 2, 3), (2, 3, 1), (2, 1, 3), (3, 4, 1), (3, 1, 4), (3, 0, 3), (4, 5, 2), (4, 2, 4), (4, 1, 5), (4, 0, 4), (5, 2, 5), (5, 1, 6), (6, 3, 2), (6, 0, 5), (7, 5, 3), (7, 2, 6), (7, 4, 2), (7, 1, 7), (7, 0, 6), (8, 5, 4), (8, 2, 7), (9, 5, 5), (9, 3, 3), (9, 0, 7), (10, 8, 0), (10, 7, 0), (10, 6, 0), (10, 9, 0), (10, 5, 6), (10, 4, 3), (10, 2, 8), (10, 3, 4), (10, 1, 8), (11, 5, 7), (11, 8, 1), (11, 7, 1), (11, 0, 8), (12, 5, 8), (12, 4, 4), (12, 6, 1), (12, 2, 9), (12, 3, 5), (12, 1, 9), (12, 0, 9), (13, 5, 9), (13, 7, 2), (13, 8, 2), (14, 4, 5), (14, 9, 1), (14, 3, 6), (14, 8, 3), (14, 7, 3), (15, 6, 2), (15, 8, 4), (15, 7, 4), (15, 4, 6), (15, 3, 7), (16, 8, 5), (16, 7, 5), (16, 6, 3), (17, 4, 7), (17, 8, 6), (17, 3, 8), (17, 7, 6), (17, 6, 4), (18, 10, 0), (18, 8, 7), (18, 3, 9), (18, 6, 5), (18, 4, 8), (18, 10, 1), (18, 6, 6), (18, 7, 7), (18, 4, 9), (18, 10, 2), (18, 6, 7), (18, 8, 8), (18, 10, 3), (18, 8, 9), (18, 7, 8), (18, 10, 4), (18, 6, 8), (18, 7, 9), (18, 6, 9), (18, 10, 5)),
+    ('yx01', 'xy01', '0xy1', 'xy01', 'yx01', 'yx01', 'xy01', '0yx1', 'x0y1'),
 )
 
 
@@ -803,16 +821,27 @@
     return jnp.sum(x, axis=0, keepdims=True)
 
 
-def ffn_kernel(
-    x, cot, ctx_a, ctx_b, ow_a, ow_b, params, small_a, small_b, uw_a, uw_b, dw_a, dw_b,
-    out, first, do_a, do_b, go_a, go_b, pre_a, pre_b, gd_all, gu_all,
-    uw, dw, act, slope, gd, gu, total, bias, bias_sum, sem_in, sem_out,
-    *, heads, chunk,
-):
+def ffn_kernel(*refs, heads, chunk, orders):
+    refs = list(refs)
+    take = lambda n: [refs.pop(0) for _ in range(n)]
+    x, cot, ctx_a, ctx_b, ow_a, ow_b, params, small_a, small_b, uw_a, uw_b, dw_a, dw_b = take(13)
+    out, first, do_a, do_b, go_a, go_b, pre_a, pre_b = take(8)
+    states = take(len(orders))
+    (gd_all,) = take(1) if not orders else (None,)
+    gu_all, uw, dw, act, slope, gd, gu, total, bias, bias_sum, sem_in, sem_out = take(12)
     width = ctx_a.shape[1]
     model = x.shape[1]
     hidden = uw_a.shape[1]
     per = hidden // chunk
+    streams = []
+    for i, order in enumerate(orders):
+        cols = model // len(orders)
+        buf, send, recv = take(3)
+        own, other = gd.at[0:hidden], gd.at[hidden : 2 * hidden]
+        columns = slice(i * cols, (i + 1) * cols)
+        streams.append(
+            stream_phases(own, other, None, None, None, columns, [buf, states[i]], send, recv, order, "head")
+        )
     for s, (u, d) in enumerate(((uw_a, dw_a), (uw_b, dw_b))):
         for i in range(per):
             n = s * per + i
@@ -823,6 +852,10 @@
             for j in range(chunk // width):
                 at = heads + 2 + i * (chunk // width) + j
                 bias[n * 8 : n * 8 + 1, j * width : (j + 1) * width] = small[at : at + 1, :]
+    if orders:
+        near = {"y": ("head", 1), "x": ("dp", 2), "0": ("dp", 4)}
+        partners = [partner("dp", 1)] + [partner(*near[axis]) for axis in sorted({order[0] for order in orders})]
+        announce(partners)
     gain1, shift1, gain2, shift2, output_shift, down_shift = (params[i : i + 1, :] for i in range(6))
 
     def put(i, vector):
@@ -863,24 +896,40 @@
     def stores(n):
         rows = pl.ds(pl.multiple_of(n * chunk, chunk), chunk)
         cols = pl.ds(pl.multiple_of(lax.rem(n, per) * chunk, chunk), chunk)
-        return (
-            pltpu.make_async_copy(gd.at[n], gd_all.at[rows], sem_out.at[n]),
-            pltpu.make_async_copy(gu.at[n], gu_all.at[lax.div(n, per), :, cols], sem_out.at[2 * per + n]),
-        )
-
-    def backward(n, _):
-        gd[n] = dot_tn(act[n], back_feed).astype(BF16)
-        stores(n)[0].start()
+        copies = [pltpu.make_async_copy(gu.at[n], gu_all.at[lax.div(n, per), :, cols], sem_out.at[n])]
+        if not orders:
+            copies.append(pltpu.make_async_copy(gd.at[rows], gd_all.at[rows], sem_out.at[2 * per + n]))
+        return copies
+
+    def backward_down(n, _):
+        gd[pl.ds(pl.multiple_of(n * chunk, chunk), chunk), :] = dot_tn(act[n], back_feed).astype(BF16)
+        return 0
+
+    def backward_up(n, _):
         back_up = (dot_nt(back_feed, dw[n]) * slope[n].astype(F32)).astype(BF16)
         bias_sum[pl.ds(pl.multiple_of(n * 8, 8), 8), :] = jnp.broadcast_to(
             row_sums(back_up.astype(F32)), (8, chunk)
         )
         gu[n] = dot_tn(low, back_up).astype(BF16)
-        stores(n)[1].start()
+        for copy in stores(n):
+            copy.start()
         total[...] += dot_nt(back_up, uw[n])
         return 0
 
-    lax.fori_loop(0, 2 * per, backward, 0)
+    def hop(i):
+        for phases in streams:
+            phases[i]()
+
+    if orders:
+        assert per == 2
+        lax.fori_loop(0, 2, lambda i, z: backward_down(2 * i + 1 - dp_bit(1), z), 0)
+        pl.semaphore_wait(pltpu.get_barrier_semaphore(), len(partners))
+        hop(0)
+        lax.fori_loop(0, 2, lambda i, z: backward_down(2 * i + dp_bit(1), z), 0)
+    else:
+        lax.fori_loop(0, 2 * per, backward_down, 0)
+    hop(1)
+    lax.fori_loop(0, 2 * per, backward_up, 0)
     for n in range(2 * per):
         for j in range(chunk // width):
             at = 6 * (model // width) + (n % per) * (chunk // width) + j
@@ -898,9 +947,11 @@
     for n in range(2 * per):
         for copy in stores(n):
             copy.wait()
-
-
-def feed_forward(x, cot, contexts, output_weights, params, smalls, up_weights, down_weights, heads, chunk=768):
+    hop(2)
+
+
+def feed_forward(x, cot, contexts, output_weights, params, smalls, up_weights, down_weights, heads, orders,
+                 collective_id, chunk=768):
     nq, model = x.shape
     width = contexts[0].shape[1]
     hidden = up_weights[0].shape[1]
@@ -909,8 +960,16 @@
     anywhere = pl.BlockSpec(memory_space=pl.ANY)
     pre_rows = 6 * (model // width) + hidden // width
     shape = jax.ShapeDtypeStruct
+    state_shapes, hop_scratch, compiler = [], [], dict(vmem_limit_bytes=VM)
+    for order in orders:
+        cols = model // len(orders)
+        state_shapes.append((1, hidden // 2, cols) if order[0] == "y" else (2, hidden // 4, cols))
+        hop_scratch.append(pltpu.VMEM((2, hidden // 2, cols), BF16))
+        hop_scratch += [pltpu.SemaphoreType.DMA((STREAM_SEMS,))] * 2
+    if orders:
+        compiler.update(collective_id=collective_id, has_side_effects=True)
     return pl.pallas_call(
-        functools.partial(ffn_kernel, heads=heads, chunk=chunk),
+        functools.partial(ffn_kernel, heads=heads, chunk=chunk, orders=orders),
         out_shape=(
             shape((nq, model), F32),
             shape((nq, model), F32),
@@ -920,25 +979,27 @@
             shape((model, width), BF16),
             shape((pre_rows, width), F32),
             shape((pre_rows, width), F32),
-            shape((2 * hidden, model), BF16),
+            *(shape(s, BF16) for s in state_shapes),
+            *((shape((2 * hidden, model), BF16),) if not orders else ()),
             shape((2, model, hidden), BF16),
         ),
         in_specs=[here] * 9 + [anywhere] * 4,
-        out_specs=(here,) * 8 + (anywhere,) * 2,
+        out_specs=(here,) * (8 + len(orders)) + (anywhere,) * (1 if orders else 2),
         scratch_shapes=[
             pltpu.VMEM((n, model, chunk), BF16),
             pltpu.VMEM((n, chunk, model), BF16),
             pltpu.VMEM((n, nq, chunk), BF16),
             pltpu.VMEM((n, nq, chunk), BF16),
-            pltpu.VMEM((n, chunk, model), BF16),
+            pltpu.VMEM((2 * hidden, model), BF16),
             pltpu.VMEM((n, model, chunk), BF16),
             pltpu.VMEM((nq, model), F32),
             pltpu.VMEM((n * 8, chunk), F32),
             pltpu.VMEM((n * 8, chunk), F32),
             pltpu.SemaphoreType.DMA((2 * n,)),
             pltpu.SemaphoreType.DMA((2 * n,)),
+            *hop_scratch,
         ],
-        compiler_params=pltpu.CompilerParams(vmem_limit_bytes=VM),
+        compiler_params=pltpu.CompilerParams(**compiler),
         cost_estimate=pl.CostEstimate(
             flops=12 * nq * model * 2 * hidden, bytes_accessed=100 * 2**20, transcendentals=nq * 4 * hidden
         ),
@@ -1134,17 +1195,15 @@
     )
     own_tokens = rows_of(tokens, head_index, share_rows)
 
-    scaled, keys, values_t, probs, contexts = [], [], [], [], []
+    scaled, keys_t, values, probs, contexts = [], [], [], [], []
     for s in range(2):
         wq, wk, wv = (project_weights[s][i * model_width : (i + 1) * model_width] for i in range(3))
         bq = smalls[s][local_heads : local_heads + 1]
         bv = smalls[s][local_heads + 1 : local_heads + 2]
         q = ((mm(own_tokens, wq) + bq) * 0.125).astype(BF16)
         q = q * jnp.array(2.0**SCALE_BITS, BF16)
-        k = mm(tokens, wk).astype(BF16)
         kt = dot_general_t(wk, tokens).astype(BF16)
         v = (mm(tokens, wv) + bv).astype(BF16)
-        vt = (dot_general_t(wv, tokens) + bv.reshape(-1, 1)).astype(BF16)
         if s == 0:
             fetch = (
                 ("small", (0, -1, -1), small),
@@ -1164,28 +1223,29 @@
             up_weights.append(fetched[0])
             down_weights.append(fetched[1])
         scaled.append(q)
-        keys.append(k)
-        values_t.append(vt)
+        keys_t.append(kt)
+        values.append(v)
         probs.append(p)
         contexts.append(context)
+    fast = lax.axis_size("dp") == 16
     (
         layer_output, back_first, back_own, back_other, out_own, out_other, pre_own, pre_other, *grads
     ) = feed_forward(
-        own_tokens, cotangent, contexts, output_weights, params, smalls, up_weights, down_weights, local_heads
+        own_tokens, cotangent, contexts, output_weights, params, smalls, up_weights, down_weights, local_heads,
+        BACK_PLAN[1][: BACK_CHUNKS[0]] if fast else (), 3,
     )
 
     sides = [
-        (scaled[s], keys[s], values_t[s], (back_own, back_other)[s], probs[s]) for s in range(2)
+        (scaled[s], keys_t[s], values[s], (back_own, back_other)[s], probs[s]) for s in range(2)
     ]
     pre = (pre_own, pre_other)
-    fast = lax.axis_size("dp") == 16
     results = attend_backward(
         sides,
         code,
         tokens.T,
         project_weights,
         bits,
-        (*grads, out_own, out_other),
+        (*(grads if fast else grads[1:]), out_own, out_other),
         pre,
         2,
         fast,

time: 276 us -> 261 us (0.946)
  Pallas kernels: 243 us -> 233 us
  matrix products: 16 us -> 12 us
    pallas_call x1, Pallas kernels: 127 us -> 113 us  [attend_backward(): pl.pallas_call(functools.partial(back_kernel, pairs=pairs, qb=qb, hb=hb,...]
    pallas_call x1, Pallas kernels: 32.5 us -> 37.6 us  [feed_forward(): pl.pallas_call(functools.partial(ffn_kernel, heads=heads, chunk=chunk, or...]
    dot_general x5 -> x4, matrix products: 10.5 us -> 8.61 us  [mm(): return jnp.dot(a, b, preferred_element_type=F32)]
where the time goes in v1:
time: 261 us; the launch traced here: 260 us
  Pallas kernels  233 us (89%)
  matrix products  12 us (5%)
  local copies, waits for them, and re-layouts  9.58 us (4%)
  other arithmetic  4.84 us (2%)
    pallas_call x1, Pallas kernels, attend_backward(): pl.pallas_call(functools.partial(back_kernel, pairs=pairs, qb=qb, hb=hb,...  113 us
    pallas_call x2, Pallas kernels, attend_fwd(): pl.pallas_call(functools.partial(fwd_kernel, pairs=pairs, qb=qb, modes=mo...  70.9 us
    pallas_call x1, Pallas kernels, feed_forward(): pl.pallas_call(functools.partial(ffn_kernel, heads=heads, chunk=chunk, or...  37.6 us
    pallas_call x1, Pallas kernels, finish(): pl.pallas_call(functools.partial(finish_kernel, count=count, heads=heads,...  12 us
    dot_general x4, matrix products, mm(): return jnp.dot(a, b, preferred_element_type=F32)  8.61 us

profile of v1, /device:TPU:0, one launch (start us, length us, event | category | flops | bytes accessed | tf_op | source)
XLA Modules:
  0.0 260.3 jit_solution(7047358390574702850)
XLA Ops:
  0.7 0.7 constant_dynamic-slice_fusion
  1.4 0.0 copy-start.6
  1.4 0.0 copy-start.7
  1.4 0.0 copy-start.8
  1.4 0.0 copy-start
  1.4 4.8 %select_add_fusion.refs_0_.refs_10_ = s32[512,1024]{1,0:T(8,128)} fusion(s32[1024,1024]{1,0:T(8,128)} %param.43, s32[]{:T(128)S(6)} %select_n.14, s32[1024,1024]{1,0:T(8,128)} %param.42, s32[1024,1024]{1,0:T(8,128)} %param.41, s32[1024]{0:T(1024)} %bitcast.50, s32[512]{0:T(512)S(1)} %bitcast.51), kind=kLoop, calls=%fused_computation | loop fusion | flops 3670016 | bytes 8394756 | tf_op jit(solution)/shard_map/add | solution.py:19
  6.3 0.9 constant_dynamic-slice_fusion.2.refs_0_
  7.3 2.5 fusion.6.refs_2_.refs_0_
  9.8 1.9 add_convert_fusion.1.refs_4_.refs_2_
  11.6 1.7 convolution_convert_fusion.1.refs_3_.refs_1_
  13.3 0.6 pad.18.refs_1_.refs_5_.refs_7_.refs_12_
  13.9 35.2 %shard_map.621 = (bf16[6,512,1024]{2,1,0:T(8,128)(2,1)}, bf16[512,384]{1,0:T(8,128)(2,1)}, f32[16,384]{1,0:T(8,128)}, bf16[2304,384]{1,0:T(8,128)(2,1)}, bf16[38...) custom-call(s32[512,1024]{1,0:T(8,128)} %select_add_fusion.refs_0_.refs_10_, ...), custom_call_target="tpu_custom_call" | custom-call | flops 805306368 | bytes 94371840 | tf_op jit(solution)/shard_map/pallas_call | solution.py:227
  49.1 0.9 slice_reduce_fusion.2
  50.0 2.4 fusion.5.refs_2_.refs_5_
  52.4 1.9 fusion.refs_4_.refs_7_
  54.3 1.7 convolution_convert_fusion.refs_3_.refs_6_
  56.0 0.0 copy-start.13
  56.0 0.0 copy-start.14
  56.1 35.8 %shard_map.622 = (bf16[6,512,1024]{2,1,0:T(8,128)(2,1)}, bf16[512,384]{1,0:T(8,128)(2,1)}, bf16[768,1536]{1,0:T(8,128)(2,1)}, bf16[1536,768]{1,0:T(8,128)(2,1)}) custom-call(s32[512,1024]{1,0:T(8,128)} %select_add_fusion.refs_0_.refs_10_, f32[16,384]{1,0:T(8,128)} %get-tuple-element.96.refs_1_.refs_8_, bf16[512,384]{1,0:T(8,128)(2,1)} %fusion.5.refs_2_.refs_5_, ...), custom_call_target="tpu_custom_call" | custom-call | flops 805306368 | bytes 94371840 | tf_op jit(solution)/shard_map/pallas_call | solution.py:227
  91.8 0.2 dynamic-update-slice
  92.1 0.2 dynamic-update-slice.1
  92.3 0.2 dynamic-update-slice.2
  92.5 0.2 dynamic-update-slice.3
  92.7 0.2 dynamic-update-slice.4
  92.9 0.2 dynamic-update-slice.5
  93.1 0.6 reshape.86.refs_6_.refs_11_
  93.8 37.6 %shard_map.623 = (f32[512,768]{1,0:T(8,128)}, f32[512,768]{1,0:T(8,128)}, bf16[512,384]{1,0:T(8,128)(2,1)}, bf16[512,384]{1,0:T(8,128)(2,1)}, bf16[768,384]{1,0:...) custom-call(bf16[512,768]{1,0:T(8,128)(2,1)} %constant_dynamic-slice, ...), custom_call_target="tpu_custom_call" | custom-call | flops 14495514624 | bytes 104857600 | tf_op jit(solution)/shard_map/pallas_call | solution.py:971
  131.4 1.6 copy.73
  133.0 112.5 %shard_map.624 = (bf16[1536,768]{1,0:T(8,128)(2,1)}, bf16[768,1536]{1,0:T(8,128)(2,1)}, bf16[768,384]{1,0:T(8,128)(2,1)}, bf16[768,1152]{1,0:T(8,128)(2,1)}, f32[768,512]{1,0:T(8,128)}, /*index=5*/f32[40,384]{1,0:T(8,128)}) custom-call(bf16[512,384]{1,0:T(8,128)(2,1)} %fusion.6.refs_2_.refs_0_, bf16[384,1024]{1,0:T(8,128)(2,1)} %convolution_convert_fusion.1.refs_3_.refs_1_, ...), custom_call_target="tpu_custom_call" | custom-call | flops 3221225472 | bytes 314572800 | tf_op jit(solution)/shard_map/pallas_call | solution.py:713
  245.5 1.7 constant_dynamic-slice_fusion.1.refs_14_
  247.2 12.0 %shard_map.625 = (f32[512,768]{1,0:T(8,128)}, f32[3,768,384]{2,1,0:T(8,128)}, f32[384]{0:T(512)}, f32[384]{0:T(512)}, f32[384,768]{1,0:T(8,128)}, /*index=5*/f32...) custom-call(s32[1]{0:T(128)} %bitcast.11.index, ...), custom_call_target="tpu_custom_call" | custom-call | flops 16777216 | bytes 41943040 | tf_op jit(solution)/shard_map/pallas_call | solution.py:1105
  259.2 1.1 copy.82
  (33 shorter events, 0.1 us)
Async XLA Ops:
  1.4 4.9 %copy-start.1 = (bf16[1024,768]{1,0:T(8,128)(2,1)S(1)}, bf16[1024,768]{1,0:T(8,128)(2,1)}, u32[]{:S(2)}) copy-start(bf16[1024,768]{1,0:T(8,128)(2,1)} %param.38) | copy-start | bytes 4718596
  1.4 5.8 %copy-start.5 = (bf16[1536]{0:T(1024)(128)(2,1)S(1)}, bf16[1536]{0:T(1024)(128)(2,1)}, u32[]{:S(2)}) copy-start(bf16[1536]{0:T(1024)(128)(2,1)} %param.52) | copy-start | bytes 9220
  1.4 5.8 %copy-start.15 = (bf16[384]{0:T(512)(128)(2,1)S(1)}, bf16[384]{0:T(512)(128)(2,1)}, u32[]{:S(2)}) copy-start(bf16[384]{0:T(512)(128)(2,1)} %param.46) | copy-start | bytes 2308
  1.4 5.8 %copy-start.16 = (bf16[384]{0:T(512)(128)(2,1)S(1)}, bf16[384]{0:T(512)(128)(2,1)}, u32[]{:S(2)}) copy-start(bf16[384]{0:T(512)(128)(2,1)} %param.45) | copy-start | bytes 2308
  1.4 5.8 %copy-start.6 = (bf16[64,6]{0,1:T(8,128)(2,1)S(1)}, bf16[64,6]{0,1:T(8,128)(2,1)}, u32[]{:S(2)}) copy-start(bf16[64,6]{0,1:T(8,128)(2,1)} %param.59) | copy-start | bytes 2308
  1.4 5.8 %copy-start.7 = (bf16[64,6]{0,1:T(8,128)(2,1)S(1)}, bf16[64,6]{0,1:T(8,128)(2,1)}, u32[]{:S(2)}) copy-start(bf16[64,6]{0,1:T(8,128)(2,1)} %param.58) | copy-start | bytes 2308
  1.4 5.8 %copy-start.8 = (bf16[32,6]{0,1:T(8,128)(2,1)S(1)}, bf16[32,6]{0,1:T(8,128)(2,1)}, u32[]{:S(2)}) copy-start(bf16[32,6]{0,1:T(8,128)(2,1)} %param.57) | copy-start | bytes 1156
  1.4 5.9 %copy-start = (bf16[768,3,384]{2,0,1:T(8,128)(2,1)S(1)}, bf16[768,3,384]{2,0,1:T(8,128)(2,1)}, u32[]{:S(2)}) copy-start(bf16[768,3,384]{2,0,1:T(8,128)(2,1)} %param.44) | copy-start | bytes 5308420
  13.9 36.0 %copy-start.4 = (bf16[512,768]{1,0:T(8,128)(2,1)S(1)}, bf16[512,768]{1,0:T(8,128)(2,1)}, u32[]{:S(2)}) copy-start(bf16[512,768]{1,0:T(8,128)(2,1)} %constant_dynamic-slice_fusion.2.refs_0_) | copy-start | bytes 2359300
  49.1 3.3 %copy-start.2 = (bf16[2304,384]{1,0:T(8,128)(2,1)S(1)}, bf16[2304,384]{1,0:T(8,128)(2,1)}, u32[]{:S(2)}) copy-start(bf16[2304,384]{1,0:T(8,128)(2,1)} %get-tuple-element.97.refs_13_) | copy-start | bytes 5308420
  56.0 35.8 %copy-start.9 = (bf16[768]{0:T(1024)(128)(2,1)S(1)}, bf16[768]{0:T(1024)(128)(2,1)}, u32[]{:S(2)}) copy-start(bf16[768]{0:T(1024)(128)(2,1)} %param.49) | copy-start | bytes 4612
  56.0 36.1 %copy-start.10 = (bf16[768]{0:T(1024)(128)(2,1)S(1)}, bf16[768]{0:T(1024)(128)(2,1)}, u32[]{:S(2)}) copy-start(bf16[768]{0:T(1024)(128)(2,1)} %param.50) | copy-start | bytes 4612
  56.0 36.3 %copy-start.11 = (bf16[768]{0:T(1024)(128)(2,1)S(1)}, bf16[768]{0:T(1024)(128)(2,1)}, u32[]{:S(2)}) copy-start(bf16[768]{0:T(1024)(128)(2,1)} %param.55) | copy-start | bytes 4612
  56.0 36.5 %copy-start.12 = (bf16[768]{0:T(1024)(128)(2,1)S(1)}, bf16[768]{0:T(1024)(128)(2,1)}, u32[]{:S(2)}) copy-start(bf16[768]{0:T(1024)(128)(2,1)} %param.56) | copy-start | bytes 4612
  56.0 36.7 %copy-start.13 = (bf16[768]{0:T(1024)(128)(2,1)S(1)}, bf16[768]{0:T(1024)(128)(2,1)}, u32[]{:S(2)}) copy-start(bf16[768]{0:T(1024)(128)(2,1)} %param.48) | copy-start | bytes 4612
  56.0 36.9 %copy-start.14 = (bf16[768]{0:T(1024)(128)(2,1)S(1)}, bf16[768]{0:T(1024)(128)(2,1)}, u32[]{:S(2)}) copy-start(bf16[768]{0:T(1024)(128)(2,1)} %param.54) | copy-start | bytes 4612
  247.2 12.0 %copy-start.3 = (f32[512,768]{1,0:T(8,128)S(1)}, f32[512,768]{1,0:T(8,128)}, u32[]{:S(2)}) copy-start(f32[512,768]{1,0:T(8,128)} %get-tuple-element.194) | copy-start | bytes 4718596

commit v2 on v1

--- a/solution.py
+++ b/solution.py
@@ -750,7 +750,7 @@
 
 def gelu_parts(u):
     t = 1.0 / (1.0 + (0.3275911 * 0.7071067811865476) * jnp.abs(u))
-    e = jnp.exp(-0.5 * u * u)
+    e = jnp.exp2((-0.5 * 1.4426950408889634) * (u * u))
     poly = t * (
         0.254829592 + t * (-0.284496736 + t * (1.421413741 + t * (-1.453152027 + t * 1.061405429)))
     )
@@ -871,18 +871,23 @@
     low = normed.astype(BF16)
     total[...] = normed + down_shift
 
-    def forward(n, _):
-        pltpu.make_async_copy(uw.at[n], uw.at[n], sem_in.at[n]).wait()
-        row = bias[pl.ds(pl.multiple_of(n * 8, 8), 8), :][0:1]
-        a, slope_n = gelu_parts(dot_nn(low, uw[n]) + row)
-        a = a.astype(BF16)
-        act[n] = a
-        slope[n] = slope_n.astype(BF16)
-        pltpu.make_async_copy(dw.at[n], dw.at[n], sem_in.at[2 * per + n]).wait()
-        total[...] += dot_nn(a, dw[n])
+    def forward(i, _):
+        both = (2 * i, 2 * i + 1)
+        for n in both:
+            pltpu.make_async_copy(uw.at[n], uw.at[n], sem_in.at[n]).wait()
+            pltpu.make_async_copy(dw.at[n], dw.at[n], sem_in.at[2 * per + n]).wait()
+        ups = [dot_nn(low, uw[n]) + bias[pl.ds(pl.multiple_of(n * 8, 8), 8), :][0:1] for n in both]
+        parts = []
+        for n, u in zip(both, ups):
+            a, slope_n = gelu_parts(u)
+            a = a.astype(BF16)
+            act[n] = a
+            slope[n] = slope_n.astype(BF16)
+            parts.append(dot_nn(a, dw[n]))
+        total[...] += parts[0] + parts[1]
         return 0
 
-    lax.fori_loop(0, 2 * per, forward, 0)
+    lax.fori_loop(0, per, forward, 0)
     n2, root2 = normalize(total[...])
     out[...] = n2 * gain2 + shift2
     g = cot[...].astype(F32)
@@ -1212,7 +1217,7 @@
                 ("first", (0, -1, -1), up_weight),
             )
         else:
-            fetch = (("rest", (-1, 0, 4), up_part), ("all", (0, 4, 8), down_weight))
+            fetch = (("rest", (-1, 0, 4), up_part), ("all", (0, 4, 7), down_weight))
         p, context, *fetched = attend_fwd(code, smalls[s], q, kt, v, fetch, s, qb=block_rows)
         if s == 0:
             smalls.append(fetched[0])

time: 261 us -> 260 us (level)
  no operation moved by 1% of the time
where the time goes in v2:
time: 260 us; the launch traced here: 259 us
  Pallas kernels  232 us (89%)
  matrix products  12 us (5%)
  local copies, waits for them, and re-layouts  9.58 us (4%)
  other arithmetic  4.84 us (2%)
    pallas_call x1, Pallas kernels, attend_backward(): pl.pallas_call(functools.partial(back_kernel, pairs=pairs, qb=qb, hb=hb,...  113 us
    pallas_call x2, Pallas kernels, attend_fwd(): pl.pallas_call(functools.partial(fwd_kernel, pairs=pairs, qb=qb, modes=mo...  70.9 us
    pallas_call x1, Pallas kernels, feed_forward(): pl.pallas_call(functools.partial(ffn_kernel, heads=heads, chunk=chunk, or...  35.9 us
    pallas_call x1, Pallas kernels, finish(): pl.pallas_call(functools.partial(finish_kernel, count=count, heads=heads,...  12 us
    dot_general x4, matrix products, mm(): return jnp.dot(a, b, preferred_element_type=F32)  8.61 us

profile of v2, /device:TPU:0, one launch (start us, length us, event | category | flops | bytes accessed | tf_op | source)
XLA Modules:
  0.0 259.1 jit_solution(5253358186939682797)
XLA Ops:
  0.7 0.7 constant_dynamic-slice_fusion
  1.4 0.0 copy-start.6
  1.4 0.0 copy-start.7
  1.4 0.0 copy-start.8
  1.4 0.0 copy-start
  1.4 4.8 %select_add_fusion.refs_0_.refs_10_ = s32[512,1024]{1,0:T(8,128)} fusion(s32[1024,1024]{1,0:T(8,128)} %param.43, s32[]{:T(128)S(6)} %select_n.14, s32[1024,1024]{1,0:T(8,128)} %param.42, s32[1024,1024]{1,0:T(8,128)} %param.41, s32[1024]{0:T(1024)} %bitcast.50, s32[512]{0:T(512)S(1)} %bitcast.51), kind=kLoop, calls=%fused_computation | loop fusion | flops 3670016 | bytes 8394756 | tf_op jit(solution)/shard_map/add | solution.py:19
  6.3 0.9 constant_dynamic-slice_fusion.2.refs_0_
  7.3 2.5 fusion.6.refs_2_.refs_0_
  9.8 1.9 add_convert_fusion.1.refs_4_.refs_2_
  11.6 1.7 convolution_convert_fusion.1.refs_3_.refs_1_
  13.3 0.6 pad.18.refs_1_.refs_5_.refs_7_.refs_12_
  13.9 35.2 %shard_map.621 = (bf16[6,512,1024]{2,1,0:T(8,128)(2,1)}, bf16[512,384]{1,0:T(8,128)(2,1)}, f32[16,384]{1,0:T(8,128)}, bf16[2304,384]{1,0:T(8,128)(2,1)}, bf16[38...) custom-call(s32[512,1024]{1,0:T(8,128)} %select_add_fusion.refs_0_.refs_10_, ...), custom_call_target="tpu_custom_call" | custom-call | flops 805306368 | bytes 94371840 | tf_op jit(solution)/shard_map/pallas_call | solution.py:227
  49.1 0.9 slice_reduce_fusion.2
  50.0 2.4 fusion.5.refs_2_.refs_5_
  52.4 1.9 fusion.refs_4_.refs_7_
  54.3 1.7 convolution_convert_fusion.refs_3_.refs_6_
  56.0 0.0 copy-start.13
  56.0 0.0 copy-start.14
  56.1 35.8 %shard_map.622 = (bf16[6,512,1024]{2,1,0:T(8,128)(2,1)}, bf16[512,384]{1,0:T(8,128)(2,1)}, bf16[768,1536]{1,0:T(8,128)(2,1)}, bf16[1536,768]{1,0:T(8,128)(2,1)}) custom-call(s32[512,1024]{1,0:T(8,128)} %select_add_fusion.refs_0_.refs_10_, f32[16,384]{1,0:T(8,128)} %get-tuple-element.96.refs_1_.refs_8_, bf16[512,384]{1,0:T(8,128)(2,1)} %fusion.5.refs_2_.refs_5_, ...), custom_call_target="tpu_custom_call" | custom-call | flops 805306368 | bytes 94371840 | tf_op jit(solution)/shard_map/pallas_call | solution.py:227
  91.8 0.2 dynamic-update-slice
  92.1 0.2 dynamic-update-slice.1
  92.3 0.2 dynamic-update-slice.2
  92.5 0.2 dynamic-update-slice.3
  92.7 0.2 dynamic-update-slice.4
  92.9 0.2 dynamic-update-slice.5
  93.1 0.6 reshape.86.refs_6_.refs_11_
  93.8 35.9 %shard_map.623 = (f32[512,768]{1,0:T(8,128)}, f32[512,768]{1,0:T(8,128)}, bf16[512,384]{1,0:T(8,128)(2,1)}, bf16[512,384]{1,0:T(8,128)(2,1)}, bf16[768,384]{1,0:...) custom-call(bf16[512,768]{1,0:T(8,128)(2,1)} %constant_dynamic-slice, ...), custom_call_target="tpu_custom_call" | custom-call | flops 14495514624 | bytes 104857600 | tf_op jit(solution)/shard_map/pallas_call | solution.py:976
  129.7 1.6 copy.73
  131.3 113.0 %shard_map.624 = (bf16[1536,768]{1,0:T(8,128)(2,1)}, bf16[768,1536]{1,0:T(8,128)(2,1)}, bf16[768,384]{1,0:T(8,128)(2,1)}, bf16[768,1152]{1,0:T(8,128)(2,1)}, f32[768,512]{1,0:T(8,128)}, /*index=5*/f32[40,384]{1,0:T(8,128)}) custom-call(bf16[512,384]{1,0:T(8,128)(2,1)} %fusion.6.refs_2_.refs_0_, bf16[384,1024]{1,0:T(8,128)(2,1)} %convolution_convert_fusion.1.refs_3_.refs_1_, ...), custom_call_target="tpu_custom_call" | custom-call | flops 3221225472 | bytes 314572800 | tf_op jit(solution)/shard_map/pallas_call | solution.py:713
  244.3 1.7 constant_dynamic-slice_fusion.1.refs_14_
  246.0 12.0 %shard_map.625 = (f32[512,768]{1,0:T(8,128)}, f32[3,768,384]{2,1,0:T(8,128)}, f32[384]{0:T(512)}, f32[384]{0:T(512)}, f32[384,768]{1,0:T(8,128)}, /*index=5*/f32...) custom-call(s32[1]{0:T(128)} %bitcast.11.index, ...), custom_call_target="tpu_custom_call" | custom-call | flops 16777216 | bytes 41943040 | tf_op jit(solution)/shard_map/pallas_call | solution.py:1110
  258.0 1.1 copy.82
  (33 shorter events, 0.1 us)
Async XLA Ops:
  1.4 4.9 %copy-start.1 = (bf16[1024,768]{1,0:T(8,128)(2,1)S(1)}, bf16[1024,768]{1,0:T(8,128)(2,1)}, u32[]{:S(2)}) copy-start(bf16[1024,768]{1,0:T(8,128)(2,1)} %param.38) | copy-start | bytes 4718596
  1.4 5.8 %copy-start.5 = (bf16[1536]{0:T(1024)(128)(2,1)S(1)}, bf16[1536]{0:T(1024)(128)(2,1)}, u32[]{:S(2)}) copy-start(bf16[1536]{0:T(1024)(128)(2,1)} %param.52) | copy-start | bytes 9220
  1.4 5.8 %copy-start.15 = (bf16[384]{0:T(512)(128)(2,1)S(1)}, bf16[384]{0:T(512)(128)(2,1)}, u32[]{:S(2)}) copy-start(bf16[384]{0:T(512)(128)(2,1)} %param.46) | copy-start | bytes 2308
  1.4 5.8 %copy-start.16 = (bf16[384]{0:T(512)(128)(2,1)S(1)}, bf16[384]{0:T(512)(128)(2,1)}, u32[]{:S(2)}) copy-start(bf16[384]{0:T(512)(128)(2,1)} %param.45) | copy-start | bytes 2308
  1.4 5.8 %copy-start.6 = (bf16[64,6]{0,1:T(8,128)(2,1)S(1)}, bf16[64,6]{0,1:T(8,128)(2,1)}, u32[]{:S(2)}) copy-start(bf16[64,6]{0,1:T(8,128)(2,1)} %param.59) | copy-start | bytes 2308
  1.4 5.8 %copy-start.7 = (bf16[64,6]{0,1:T(8,128)(2,1)S(1)}, bf16[64,6]{0,1:T(8,128)(2,1)}, u32[]{:S(2)}) copy-start(bf16[64,6]{0,1:T(8,128)(2,1)} %param.58) | copy-start | bytes 2308
  1.4 5.8 %copy-start.8 = (bf16[32,6]{0,1:T(8,128)(2,1)S(1)}, bf16[32,6]{0,1:T(8,128)(2,1)}, u32[]{:S(2)}) copy-start(bf16[32,6]{0,1:T(8,128)(2,1)} %param.57) | copy-start | bytes 1156
  1.4 5.9 %copy-start = (bf16[768,3,384]{2,0,1:T(8,128)(2,1)S(1)}, bf16[768,3,384]{2,0,1:T(8,128)(2,1)}, u32[]{:S(2)}) copy-start(bf16[768,3,384]{2,0,1:T(8,128)(2,1)} %param.44) | copy-start | bytes 5308420
  13.9 36.0 %copy-start.4 = (bf16[512,768]{1,0:T(8,128)(2,1)S(1)}, bf16[512,768]{1,0:T(8,128)(2,1)}, u32[]{:S(2)}) copy-start(bf16[512,768]{1,0:T(8,128)(2,1)} %constant_dynamic-slice_fusion.2.refs_0_) | copy-start | bytes 2359300
  49.1 3.3 %copy-start.2 = (bf16[2304,384]{1,0:T(8,128)(2,1)S(1)}, bf16[2304,384]{1,0:T(8,128)(2,1)}, u32[]{:S(2)}) copy-start(bf16[2304,384]{1,0:T(8,128)(2,1)} %get-tuple-element.97.refs_13_) | copy-start | bytes 5308420
  56.0 35.8 %copy-start.9 = (bf16[768]{0:T(1024)(128)(2,1)S(1)}, bf16[768]{0:T(1024)(128)(2,1)}, u32[]{:S(2)}) copy-start(bf16[768]{0:T(1024)(128)(2,1)} %param.49) | copy-start | bytes 4612
  56.0 36.1 %copy-start.10 = (bf16[768]{0:T(1024)(128)(2,1)S(1)}, bf16[768]{0:T(1024)(128)(2,1)}, u32[]{:S(2)}) copy-start(bf16[768]{0:T(1024)(128)(2,1)} %param.50) | copy-start | bytes 4612
  56.0 36.3 %copy-start.11 = (bf16[768]{0:T(1024)(128)(2,1)S(1)}, bf16[768]{0:T(1024)(128)(2,1)}, u32[]{:S(2)}) copy-start(bf16[768]{0:T(1024)(128)(2,1)} %param.55) | copy-start | bytes 4612
  56.0 36.5 %copy-start.12 = (bf16[768]{0:T(1024)(128)(2,1)S(1)}, bf16[768]{0:T(1024)(128)(2,1)}, u32[]{:S(2)}) copy-start(bf16[768]{0:T(1024)(128)(2,1)} %param.56) | copy-start | bytes 4612
  56.0 36.7 %copy-start.13 = (bf16[768]{0:T(1024)(128)(2,1)S(1)}, bf16[768]{0:T(1024)(128)(2,1)}, u32[]{:S(2)}) copy-start(bf16[768]{0:T(1024)(128)(2,1)} %param.48) | copy-start | bytes 4612
  56.0 36.9 %copy-start.14 = (bf16[768]{0:T(1024)(128)(2,1)S(1)}, bf16[768]{0:T(1024)(128)(2,1)}, u32[]{:S(2)}) copy-start(bf16[768]{0:T(1024)(128)(2,1)} %param.54) | copy-start | bytes 4612
  246.0 12.0 %copy-start.3 = (f32[512,768]{1,0:T(8,128)S(1)}, f32[512,768]{1,0:T(8,128)}, u32[]{:S(2)}) copy-start(f32[512,768]{1,0:T(8,128)} %get-tuple-element.194) | copy-start | bytes 4718596

commit v3 on v2

--- a/solution.py
+++ b/solution.py
@@ -1217,7 +1217,7 @@
                 ("first", (0, -1, -1), up_weight),
             )
         else:
-            fetch = (("rest", (-1, 0, 4), up_part), ("all", (0, 4, 7), down_weight))
+            fetch = (("rest", (-1, 0, 4), up_part), ("all", (0, 3, 7), down_weight))
         p, context, *fetched = attend_fwd(code, smalls[s], q, kt, v, fetch, s, qb=block_rows)
         if s == 0:
             smalls.append(fetched[0])

time: 260 us -> 260 us (level)
  no operation moved by 1% of the time
where the time goes in v3:
time: 260 us; the launch traced here: 259 us
  Pallas kernels  232 us (89%)
  matrix products  12 us (5%)
  local copies, waits for them, and re-layouts  9.58 us (4%)
  other arithmetic  4.84 us (2%)
    pallas_call x1, Pallas kernels, attend_backward(): pl.pallas_call(functools.partial(back_kernel, pairs=pairs, qb=qb, hb=hb,...  113 us
    pallas_call x2, Pallas kernels, attend_fwd(): pl.pallas_call(functools.partial(fwd_kernel, pairs=pairs, qb=qb, modes=mo...  70.9 us
    pallas_call x1, Pallas kernels, feed_forward(): pl.pallas_call(functools.partial(ffn_kernel, heads=heads, chunk=chunk, or...  35.9 us
    pallas_call x1, Pallas kernels, finish(): pl.pallas_call(functools.partial(finish_kernel, count=count, heads=heads,...  12 us
    dot_general x4, matrix products, mm(): return jnp.dot(a, b, preferred_element_type=F32)  8.61 us

profile of v3, /device:TPU:0, one launch (start us, length us, event | category | flops | bytes accessed | tf_op | source)
XLA Modules:
  0.0 259.1 jit_solution(2205209414776690706)
XLA Ops:
  0.7 0.7 constant_dynamic-slice_fusion
  1.4 0.0 copy-start.6
  1.4 0.0 copy-start.7
  1.4 0.0 copy-start.8
  1.4 0.0 copy-start
  1.4 4.8 %select_add_fusion.refs_0_.refs_10_ = s32[512,1024]{1,0:T(8,128)} fusion(s32[1024,1024]{1,0:T(8,128)} %param.43, s32[]{:T(128)S(6)} %select_n.14, s32[1024,1024]{1,0:T(8,128)} %param.42, s32[1024,1024]{1,0:T(8,128)} %param.41, s32[1024]{0:T(1024)} %bitcast.50, s32[512]{0:T(512)S(1)} %bitcast.51), kind=kLoop, calls=%fused_computation | loop fusion | flops 3670016 | bytes 8394756 | tf_op jit(solution)/shard_map/add | solution.py:19
  6.3 0.9 constant_dynamic-slice_fusion.2.refs_0_
  7.3 2.5 fusion.6.refs_2_.refs_0_
  9.8 1.9 add_convert_fusion.1.refs_4_.refs_2_
  11.6 1.7 convolution_convert_fusion.1.refs_3_.refs_1_
  13.3 0.6 pad.18.refs_1_.refs_5_.refs_7_.refs_12_
  13.9 35.2 %shard_map.621 = (bf16[6,512,1024]{2,1,0:T(8,128)(2,1)}, bf16[512,384]{1,0:T(8,128)(2,1)}, f32[16,384]{1,0:T(8,128)}, bf16[2304,384]{1,0:T(8,128)(2,1)}, bf16[38...) custom-call(s32[512,1024]{1,0:T(8,128)} %select_add_fusion.refs_0_.refs_10_, ...), custom_call_target="tpu_custom_call" | custom-call | flops 805306368 | bytes 94371840 | tf_op jit(solution)/shard_map/pallas_call | solution.py:227
  49.1 0.9 slice_reduce_fusion.2
  50.0 2.4 fusion.5.refs_2_.refs_5_
  52.4 1.9 fusion.refs_4_.refs_7_
  54.3 1.7 convolution_convert_fusion.refs_3_.refs_6_
  56.0 0.0 copy-start.13
  56.0 0.0 copy-start.14
  56.1 35.8 %shard_map.622 = (bf16[6,512,1024]{2,1,0:T(8,128)(2,1)}, bf16[512,384]{1,0:T(8,128)(2,1)}, bf16[768,1536]{1,0:T(8,128)(2,1)}, bf16[1536,768]{1,0:T(8,128)(2,1)}) custom-call(s32[512,1024]{1,0:T(8,128)} %select_add_fusion.refs_0_.refs_10_, f32[16,384]{1,0:T(8,128)} %get-tuple-element.96.refs_1_.refs_8_, bf16[512,384]{1,0:T(8,128)(2,1)} %fusion.5.refs_2_.refs_5_, ...), custom_call_target="tpu_custom_call" | custom-call | flops 805306368 | bytes 94371840 | tf_op jit(solution)/shard_map/pallas_call | solution.py:227
  91.8 0.2 dynamic-update-slice
  92.1 0.2 dynamic-update-slice.1
  92.3 0.2 dynamic-update-slice.2
  92.5 0.2 dynamic-update-slice.3
  92.7 0.2 dynamic-update-slice.4
  92.9 0.2 dynamic-update-slice.5
  93.1 0.6 reshape.86.refs_6_.refs_11_
  93.8 35.9 %shard_map.623 = (f32[512,768]{1,0:T(8,128)}, f32[512,768]{1,0:T(8,128)}, bf16[512,384]{1,0:T(8,128)(2,1)}, bf16[512,384]{1,0:T(8,128)(2,1)}, bf16[768,384]{1,0:...) custom-call(bf16[512,768]{1,0:T(8,128)(2,1)} %constant_dynamic-slice, ...), custom_call_target="tpu_custom_call" | custom-call | flops 14495514624 | bytes 104857600 | tf_op jit(solution)/shard_map/pallas_call | solution.py:976
  129.7 1.6 copy.73
  131.3 113.0 %shard_map.624 = (bf16[1536,768]{1,0:T(8,128)(2,1)}, bf16[768,1536]{1,0:T(8,128)(2,1)}, bf16[768,384]{1,0:T(8,128)(2,1)}, bf16[768,1152]{1,0:T(8,128)(2,1)}, f32[768,512]{1,0:T(8,128)}, /*index=5*/f32[40,384]{1,0:T(8,128)}) custom-call(bf16[512,384]{1,0:T(8,128)(2,1)} %fusion.6.refs_2_.refs_0_, bf16[384,1024]{1,0:T(8,128)(2,1)} %convolution_convert_fusion.1.refs_3_.refs_1_, ...), custom_call_target="tpu_custom_call" | custom-call | flops 3221225472 | bytes 314572800 | tf_op jit(solution)/shard_map/pallas_call | solution.py:713
  244.3 1.7 constant_dynamic-slice_fusion.1.refs_14_
  246.0 12.0 %shard_map.625 = (f32[512,768]{1,0:T(8,128)}, f32[3,768,384]{2,1,0:T(8,128)}, f32[384]{0:T(512)}, f32[384]{0:T(512)}, f32[384,768]{1,0:T(8,128)}, /*index=5*/f32...) custom-call(s32[1]{0:T(128)} %bitcast.11.index, ...), custom_call_target="tpu_custom_call" | custom-call | flops 16777216 | bytes 41943040 | tf_op jit(solution)/shard_map/pallas_call | solution.py:1110
  258.0 1.1 copy.82
  (33 shorter events, 0.1 us)
Async XLA Ops:
  1.4 4.9 %copy-start.1 = (bf16[1024,768]{1,0:T(8,128)(2,1)S(1)}, bf16[1024,768]{1,0:T(8,128)(2,1)}, u32[]{:S(2)}) copy-start(bf16[1024,768]{1,0:T(8,128)(2,1)} %param.38) | copy-start | bytes 4718596
  1.4 5.8 %copy-start.5 = (bf16[1536]{0:T(1024)(128)(2,1)S(1)}, bf16[1536]{0:T(1024)(128)(2,1)}, u32[]{:S(2)}) copy-start(bf16[1536]{0:T(1024)(128)(2,1)} %param.52) | copy-start | bytes 9220
  1.4 5.8 %copy-start.15 = (bf16[384]{0:T(512)(128)(2,1)S(1)}, bf16[384]{0:T(512)(128)(2,1)}, u32[]{:S(2)}) copy-start(bf16[384]{0:T(512)(128)(2,1)} %param.46) | copy-start | bytes 2308
  1.4 5.8 %copy-start.16 = (bf16[384]{0:T(512)(128)(2,1)S(1)}, bf16[384]{0:T(512)(128)(2,1)}, u32[]{:S(2)}) copy-start(bf16[384]{0:T(512)(128)(2,1)} %param.45) | copy-start | bytes 2308
  1.4 5.8 %copy-start.6 = (bf16[64,6]{0,1:T(8,128)(2,1)S(1)}, bf16[64,6]{0,1:T(8,128)(2,1)}, u32[]{:S(2)}) copy-start(bf16[64,6]{0,1:T(8,128)(2,1)} %param.59) | copy-start | bytes 2308
  1.4 5.8 %copy-start.7 = (bf16[64,6]{0,1:T(8,128)(2,1)S(1)}, bf16[64,6]{0,1:T(8,128)(2,1)}, u32[]{:S(2)}) copy-start(bf16[64,6]{0,1:T(8,128)(2,1)} %param.58) | copy-start | bytes 2308
  1.4 5.8 %copy-start.8 = (bf16[32,6]{0,1:T(8,128)(2,1)S(1)}, bf16[32,6]{0,1:T(8,128)(2,1)}, u32[]{:S(2)}) copy-start(bf16[32,6]{0,1:T(8,128)(2,1)} %param.57) | copy-start | bytes 1156
  1.4 5.9 %copy-start = (bf16[768,3,384]{2,0,1:T(8,128)(2,1)S(1)}, bf16[768,3,384]{2,0,1:T(8,128)(2,1)}, u32[]{:S(2)}) copy-start(bf16[768,3,384]{2,0,1:T(8,128)(2,1)} %param.44) | copy-start | bytes 5308420
  13.9 36.0 %copy-start.4 = (bf16[512,768]{1,0:T(8,128)(2,1)S(1)}, bf16[512,768]{1,0:T(8,128)(2,1)}, u32[]{:S(2)}) copy-start(bf16[512,768]{1,0:T(8,128)(2,1)} %constant_dynamic-slice_fusion.2.refs_0_) | copy-start | bytes 2359300
  49.1 3.3 %copy-start.2 = (bf16[2304,384]{1,0:T(8,128)(2,1)S(1)}, bf16[2304,384]{1,0:T(8,128)(2,1)}, u32[]{:S(2)}) copy-start(bf16[2304,384]{1,0:T(8,128)(2,1)} %get-tuple-element.97.refs_13_) | copy-start | bytes 5308420
  56.0 35.8 %copy-start.9 = (bf16[768]{0:T(1024)(128)(2,1)S(1)}, bf16[768]{0:T(1024)(128)(2,1)}, u32[]{:S(2)}) copy-start(bf16[768]{0:T(1024)(128)(2,1)} %param.49) | copy-start | bytes 4612
  56.0 36.1 %copy-start.10 = (bf16[768]{0:T(1024)(128)(2,1)S(1)}, bf16[768]{0:T(1024)(128)(2,1)}, u32[]{:S(2)}) copy-start(bf16[768]{0:T(1024)(128)(2,1)} %param.50) | copy-start | bytes 4612
  56.0 36.3 %copy-start.11 = (bf16[768]{0:T(1024)(128)(2,1)S(1)}, bf16[768]{0:T(1024)(128)(2,1)}, u32[]{:S(2)}) copy-start(bf16[768]{0:T(1024)(128)(2,1)} %param.55) | copy-start | bytes 4612
  56.0 36.5 %copy-start.12 = (bf16[768]{0:T(1024)(128)(2,1)S(1)}, bf16[768]{0:T(1024)(128)(2,1)}, u32[]{:S(2)}) copy-start(bf16[768]{0:T(1024)(128)(2,1)} %param.56) | copy-start | bytes 4612
  56.0 36.7 %copy-start.13 = (bf16[768]{0:T(1024)(128)(2,1)S(1)}, bf16[768]{0:T(1024)(128)(2,1)}, u32[]{:S(2)}) copy-start(bf16[768]{0:T(1024)(128)(2,1)} %param.48) | copy-start | bytes 4612
  56.0 36.9 %copy-start.14 = (bf16[768]{0:T(1024)(128)(2,1)S(1)}, bf16[768]{0:T(1024)(128)(2,1)}, u32[]{:S(2)}) copy-start(bf16[768]{0:T(1024)(128)(2,1)} %param.54) | copy-start | bytes 4612
  246.0 12.0 %copy-start.3 = (f32[512,768]{1,0:T(8,128)S(1)}, f32[512,768]{1,0:T(8,128)}, u32[]{:S(2)}) copy-start(f32[512,768]{1,0:T(8,128)} %get-tuple-element.194) | copy-start | bytes 4718596
